TPU v7x, 256 devices: a whole 4x4x8 slice. The times are simulated.
256 devices in a mesh: seq: 32 (over x, z), head: 8 (over y, core).
Axes of the slice: x: 4, y: 4, z: 8, core: 2. Of those that a mesh axis runs over, the one named last changes fastest.
Arguments:
- queries: bfloat16 [256, 64, 128], P('seq', 'head'), may hold values from -150 to 150, as said below
- prompt_keys: bfloat16 [131072, 8, 128], P('seq', 'head'), may hold values from -6 to 6
- prompt_values: bfloat16 [131072, 8, 128], P('seq', 'head'), may hold values from -6 to 6
- suffix_keys: bfloat16 [256, 512, 8, 128], P('seq', None, 'head'), may hold values from -9 to 9
- suffix_values: bfloat16 [256, 512, 8, 128], P('seq', None, 'head'), may hold values from -6 to 6
- new_keys: bfloat16 [256, 8, 128], P('seq', 'head'), may hold values from -9 to 9
- new_values: bfloat16 [256, 8, 128], P('seq', 'head'), may hold values from -6 to 6
- suffix_len: int32 [256], P('seq'), may hold values from 1 to 511, as said below
- ancestors: int32 [256], P('seq'), may hold values from 0 to 255, as said below
Outputs:
- attended: bfloat16 [256, 8192], P('seq', 'head')
- next_keys: bfloat16 [256, 512, 8, 128], P('seq', None, 'head')
- next_values: bfloat16 [256, 512, 8, 128], P('seq', None, 'head')
Inputs may be any that keep to these rules, and one draw needn't show every extreme that they name: `queries`: queries are of order a few; the range is wide. `suffix_len`: at least one particle has generated exactly 511 tokens and one exactly 1. ancestors[q] differs from q by at most 4, and by exactly 4 for some q. In every aligned block of 8 particles, the first descends from a particle of the block below and the last from a particle of the block above, where such a block exists.
All inputs are finite; a program needn't handle non-finite values.
Results may differ from a plain program's by a relative error of at most 0.0024.
Values may be sent and summed in bfloat16 or wider, within the bound.
A program may use at most 192 MiB of HBM per device.

v0:
```python
import math

import jax
import jax.numpy as jnp
from jax import lax
from jax.sharding import PartitionSpec as P


def from_behind(value, axis, steps):
    count = lax.axis_size(axis)
    leading, last = (max(0, -steps), min(count, count - steps))
    return lax.ppermute(value, axis, [(source, source + steps) for source in range(leading, last)])


def on_device(
    queries,
    prompt_keys,
    prompt_values,
    suffix_keys,
    suffix_values,
    new_keys,
    new_values,
    suffix_len,
    ancestors,
):
    own_count, local_heads, head_size = queries.shape
    kv_local = prompt_keys.shape[1]
    group = local_heads // kv_local
    score_scale = 1.0 / math.sqrt(head_size)
    all_particles_view = lax.all_gather(queries, "seq", axis=0, tiled=True)
    total_rows = all_particles_view.shape[0]
    all_particles_view = all_particles_view.reshape(total_rows, kv_local, group, head_size)
    local_len = prompt_keys.shape[0]
    block = min(local_len, 2048)
    key_blocks = prompt_keys.reshape(local_len // block, block, kv_local, head_size)
    value_blocks = prompt_values.reshape(local_len // block, block, kv_local, head_size)

    def visit(carry, pair):
        maxima, totals, weighted = carry
        block_of_keys, value_block = pair
        scores = (
            jnp.einsum(
                "vmfu,zmu->vmfz",
                all_particles_view,
                block_of_keys,
                preferred_element_type=jnp.float32,
            )
            * score_scale
        )
        block_max = jnp.max(scores, axis=3)
        weights = jnp.exp(scores - block_max[..., None])
        block_sum = jnp.sum(weights, axis=3)
        block_out = jnp.einsum(
            "yvho,ovq->yvhq",
            weights.astype(jnp.bfloat16),
            value_block,
            preferred_element_type=jnp.float32,
        )
        merged = jnp.maximum(maxima, block_max)
        old_factor = jnp.exp(maxima - merged)
        new_factor = jnp.exp(block_max - merged)
        return (
            (
                merged,
                totals * old_factor + block_sum * new_factor,
                weighted * old_factor[..., None] + block_out * new_factor[..., None],
            ),
            None,
        )

    row_shape = (total_rows, kv_local, group)
    start_state = (
        jnp.full(row_shape, -1e30, jnp.float32),
        jnp.zeros(row_shape, jnp.float32),
        jnp.zeros(row_shape + (head_size,), jnp.float32),
    )
    (maxima, totals, weighted), _ = lax.scan(visit, start_state, (key_blocks, value_blocks))
    first_row = lax.axis_index("seq") * own_count
    global_max = lax.pmax(maxima, "seq")
    factor = jnp.exp(maxima - global_max)
    own_sum, own_out = (
        lax.psum_scatter(totals * factor, "seq", scatter_dimension=0, tiled=True),
        lax.psum_scatter(weighted * factor[..., None], "seq", scatter_dimension=0, tiled=True),
    )
    own_max = lax.dynamic_slice_in_dim(global_max, first_row, own_count, 0)
    own_queries = queries.reshape(own_count, kv_local, group, head_size)
    slots = jnp.arange(suffix_keys.shape[1], dtype=jnp.int32)
    live = slots[None, :] < suffix_len[:, None]
    suffix_score_rows = (
        jnp.einsum("pkgd,pskd->pkgs", own_queries, suffix_keys, preferred_element_type=jnp.float32)
        * score_scale
    )
    nscore = (
        jnp.einsum("pkgd,pkd->pkg", own_queries, new_keys, preferred_element_type=jnp.float32)
        * score_scale
    )
    live_mask = live[:, None, None, :]
    masked = jnp.where(live_mask, suffix_score_rows, jnp.float32(-1e30))
    suffix_max = jnp.maximum(jnp.max(masked, axis=3), nscore)
    sweights = jnp.where(
        live_mask, jnp.exp(suffix_score_rows - suffix_max[..., None]), jnp.float32(0.0)
    )
    nweight = jnp.exp(nscore - suffix_max)
    suffix_sum = jnp.sum(sweights, axis=3) + nweight
    suffix_out = jnp.einsum(
        "pkgs,pskd->pkgd",
        sweights.astype(jnp.bfloat16),
        suffix_values,
        preferred_element_type=jnp.float32,
    )
    nrounded = lax.optimization_barrier(nweight.astype(jnp.bfloat16)).astype(jnp.float32)
    suffix_out = suffix_out + nrounded[..., None] * new_values.astype(jnp.float32)[:, :, None, :]
    top = jnp.maximum(own_max, suffix_max)
    first = jnp.exp(own_max - top)
    second = jnp.exp(suffix_max - top)
    denom = own_sum * first + suffix_sum * second
    combined = (own_out * first[..., None] + suffix_out * second[..., None]) / denom[..., None]
    attended = combined.reshape(own_count, local_heads * head_size).astype(jnp.bfloat16)
    here = slots[None, :] == suffix_len[:, None]
    zero = jnp.zeros((), jnp.bfloat16)
    updated_keys = jnp.where(
        here[:, :, None, None],
        new_keys[:, None],
        jnp.where(live[:, :, None, None], suffix_keys, zero),
    )
    updated_values = jnp.where(
        here[:, :, None, None],
        new_values[:, None],
        jnp.where(live[:, :, None, None], suffix_values, zero),
    )
    stacked = jnp.stack((updated_keys, updated_values))
    below = from_behind(stacked, "seq", 1)
    above = from_behind(stacked, "seq", -1)
    extended = jnp.concatenate((below, stacked, above), axis=1)
    anchor = first_row - own_count
    local_index = ancestors - anchor
    moved = jnp.take(extended, local_index, axis=1)
    return (attended, moved[0], moved[1])


def solution(mesh):
    in_specs = (
        P("seq", "head", None),
        P("seq", "head", None),
        P("seq", "head", None),
        P("seq", None, "head", None),
        P("seq", None, "head", None),
        P("seq", "head", None),
        P("seq", "head", None),
        P("seq"),
        P("seq"),
    )
    out_specs = (P("seq", "head"), P("seq", None, "head", None), P("seq", None, "head", None))
    return jax.shard_map(
        on_device, mesh=mesh, in_specs=in_specs, out_specs=out_specs, check_vma=False
    )
```

profile of v0, /device:TPU:120, one launch (start us, length us, event | category | flops | bytes accessed | tf_op | source)
XLA Modules:
  0.0 466.4 jit_solution(5774480711838669298)
XLA Ops:
  7.2 0.7 iota_compare_fusion
  8.0 3.2 fusion.40
  11.2 1.7 pad_maximum_fusion
  12.8 5.0 %collective-permute-start = (bf16[2,8,512,1,128]{4,2,1,0,3:T(8,128)(2,1)}, bf16[2,8,512,1,128]{4,2,1,0,3:T(8,128)(2,1)}, u32[]{:S(2)}, u32[]{:S(2)}) collective-permute-start(bf16[2,8,512,1,128]{4,2,1,0,3:T(8,128)(2,1)} %pad_maximum_fusion), channel_id=1, source_target_pairs={{0,8},{8,16},{16,24},{24,32},{32,40},{40,48},{48,56},{56,64},{64,7... | collective-permute-start | bytes 6291464 | tf_op jit(solution)/shard_map/ppermute | solution.py:12
  17.9 1.9 collective-permute-start.1
  19.9 92.3 %all_gather.3 = bf16[256,8,128]{2,0,1:T(8,128)(2,1)S(1)} all-gather(bf16[8,8,128]{2,0,1:T(8,128)(2,1)S(1)} %copy.47), channel_id=1, replica_groups=mesh['seq'=32,'head'=8] {'seq'}, dimensions={0}, use_global_device_ids=true | all-gather | bytes 540672 | tf_op jit(solution)/shard_map/all_gather | solution.py:30
  112.2 50.5 %while.15 = (s32[]{:T(128)}, f32[256,1,8]{0,2,1:T(8,128)S(1)}, f32[256,1,8]{0,2,1:T(8,128)S(1)}, f32[256,1,8,128]{0,3,2,1:T(8,128)S(1)}, bf16[2,2048,1,128]{3,1,...) while((s32[]{:T(128)}, f32[256,1,8]{0,2,1:T(8,128)S(1)}, ...), condition=%wide.region_3.4_spmd.clone, body=%wide.region_0.3_spmd.clone.sunk | while | flops 2182103040 | bytes 58352260 | solution.py:77
  112.2 9.1 %bitcast_reduce_fusion.2 = (f32[256,8]{0,1:T(8,128)S(1)}, f32[2048,256,8]{1,0,2:T(8,128)}) fusion(bf16[256,1,8,128]{3,0,2,1:T(8,128)(2,1)S(1)} %get-tuple-element.214, bf16[2,2048,1,128]{3,1,2,0:T(8,128)(2,1)} %get-tuple-element.213, s32[]{:T(128)} %get-tuple-element.200), kind=kOutput, calls=%fused_computation.2.clone.1 | convolution fusion | flops 1082128384 | bytes 17834496 | tf_op jit(solution)/shard_map/while/body/eval_jaxpr/vmfu,zmu->vmfz/dot_general | solution.py:42
  121.3 8.6 %fusion.69 = f32[256,8]{0,1:T(8,128)S(1)} fusion(f32[2048,256,8]{1,0,2:T(8,128)} %get-tuple-element.187, f32[256,8]{0,1:T(8,128)S(1)} %get-tuple-element.185), kind=kLoop, calls=%fused_computation.5.clone.1 | loop fusion | flops 12580864 | bytes 16793600 | tf_op jit(solution)/shard_map/while/body/eval_jaxpr/reduce_sum | solution.py:52
  129.9 7.5 %fusion.71 = f32[256,1,8,128]{0,3,2,1:T(8,128)S(1)} fusion(f32[2048,256,8]{1,0,2:T(8,128)} %get-tuple-element.187, f32[256,8]{0,1:T(8,128)S(1)} %get-tuple-element.185, f32[256,1,8,128]{0,3,2,1:T(8,128)S(1)} %get-tuple-element.203, f32[256,8]{0,1:T(8,128)S(1)} %get-tuple-element.189, bf16[2,2048,1,128]{3,1,0,2:T(8,128)(2,1)S(1)} %copy-done.2, ...), kind=kOutput, calls=%fused_computation.11.clone.1 | convolution fusion | flops 1087373312 | bytes 19423236 | tf_op jit(solution)/shard_map/while/body/eval_jaxpr/yvho,ovq->yvhq/dot_general | solution.py:53
  137.4 9.1 %bitcast_reduce_fusion.2 = (f32[256,8]{0,1:T(8,128)S(1)}, f32[2048,256,8]{1,0,2:T(8,128)}) fusion(bf16[256,1,8,128]{3,0,2,1:T(8,128)(2,1)S(1)} %get-tuple-element.214, bf16[2,2048,1,128]{3,1,2,0:T(8,128)(2,1)} %get-tuple-element.213, s32[]{:T(128)} %get-tuple-element.200), kind=kOutput, calls=%fused_computation.2.clone.1 | convolution fusion | flops 1082128384 | bytes 17834496 | tf_op jit(solution)/shard_map/while/body/eval_jaxpr/vmfu,zmu->vmfz/dot_general | solution.py:42
  146.5 8.6 %fusion.69 = f32[256,8]{0,1:T(8,128)S(1)} fusion(f32[2048,256,8]{1,0,2:T(8,128)} %get-tuple-element.187, f32[256,8]{0,1:T(8,128)S(1)} %get-tuple-element.185), kind=kLoop, calls=%fused_computation.5.clone.1 | loop fusion | flops 12580864 | bytes 16793600 | tf_op jit(solution)/shard_map/while/body/eval_jaxpr/reduce_sum | solution.py:52
  155.1 7.5 %fusion.71 = f32[256,1,8,128]{0,3,2,1:T(8,128)S(1)} fusion(f32[2048,256,8]{1,0,2:T(8,128)} %get-tuple-element.187, f32[256,8]{0,1:T(8,128)S(1)} %get-tuple-element.185, f32[256,1,8,128]{0,3,2,1:T(8,128)S(1)} %get-tuple-element.203, f32[256,8]{0,1:T(8,128)S(1)} %get-tuple-element.189, bf16[2,2048,1,128]{3,1,0,2:T(8,128)(2,1)S(1)} %copy-done.2, ...), kind=kOutput, calls=%fused_computation.11.clone.1 | convolution fusion | flops 1087373312 | bytes 19423236 | tf_op jit(solution)/shard_map/while/body/eval_jaxpr/yvho,ovq->yvhq/dot_general | solution.py:53
  162.7 66.2 %pmax.7 = f32[256,1,8]{0,2,1:T(8,128)S(1)} all-reduce(f32[256,1,8]{0,2,1:T(8,128)S(1)} %get-tuple-element.43), channel_id=1, replica_groups=mesh['seq'=32,'head'=8] {'seq'}, use_global_device_ids=true, to_apply=%region_4.5 | all-reduce | flops 2048 | bytes 16384 | tf_op jit(solution)/shard_map/pmax | solution.py:79
  228.9 0.1 copy.49
  229.1 1.3 copy.50
  230.4 2.6 broadcast_multiply_fusion
  233.0 1.7 select_reduce_fusion
  234.7 0.1 fusion.51
  234.9 0.2 fusion.43
  235.1 0.1 copy.55
  235.3 0.6 dynamic-slice
  236.5 137.2 %all-reduce = f32[256,1,8]{2,0,1:T(8,128)S(1)} all-reduce(f32[256,1,8]{2,0,1:T(8,128)S(1)} %copy.55), channel_id=3, replica_groups=mesh['seq'=32,'head'=8] {'seq'}, use_global_device_ids=true, to_apply=%region_7.8.clone | all-reduce | flops 2048 | bytes 16384
  373.7 0.1 copy.56
  373.8 0.1 multiply_add_fusion
  374.2 72.2 %reduce-scatter.3.cloned.1.call-done = f32[8,1,8,128]{3,2,0,1:T(8,128)} async-done(((f32[256,1,8,128]{3,2,0,1:T(8,128)}), f32[8,1,8,128]{3,2,0,1:T(8,128)}) %reduce-scatter.3.cloned.1.call-update) | async-done | bytes 32784 | tf_op jit(solution)/shard_map/reduce_scatter | solution.py:83
  446.4 1.5 fusion.36
  448.0 0.6 copy.74
  448.6 5.5 %maximum_bitcast_fusion = bf16[2,24,512,128]{3,2,1,0:T(8,128)(2,1)} fusion(bf16[2,8,512,1,128]{4,2,1,0,3:T(8,128)(2,1)} %collective-permute-done.1, bf16[1,8,512,1,128]{4,2,1,0,3:T(8,128)(2,1)S(1)} %copy-done.1, bf16[1,8,512,1,128]{4,2,1,0,3:T(8,128)(2,1)S(1)} %get-tuple-element.130, bf16[2,8,512,1,128]{4,2,1,0,3:T(8,128)(2,1)} %collective-permute-done), kind=kLoop, calls=%fused_computation.31 | loop fusion | flops 9437184 | bytes 12582912 | tf_op jit(solution)/shard_map/concatenate | solution.py:134
  454.1 3.7 gather_fusion
  457.9 0.3 bitcast_select_fusion
  458.1 1.5 slice_bitcast_fusion
  (45 shorter events, 0.6 us)
Async XLA Ops:
  7.2 12.7 %copy-start.3 = (bf16[8,8,128]{2,1,0:T(8,128)(2,1)S(1)}, bf16[8,8,128]{2,1,0:T(8,128)(2,1)}, u32[]{:S(2)}) copy-start(bf16[8,8,128]{2,1,0:T(8,128)(2,1)} %param.11) | copy-start | bytes 49156
  7.2 439.3 %reduce-scatter.3.cloned.1.call-start = ((), (), s32[]{:S(2)}) async-start(), calls=%async_computation.1 | async-start | bytes 1081344 | tf_op jit(solution)/shard_map/reduce_scatter | solution.py:83
  11.2 6.7 %copy-start = (bf16[1,8,512,1,128]{4,2,1,0,3:T(8,128)(2,1)}, bf16[1,8,512,1,128]{4,2,1,0,3:T(8,128)(2,1)S(1)}, u32[]{:S(2)}) copy-start(bf16[1,8,512,1,128]{4,2,1,0,3:T(8,128)(2,1)S(1)} %get-tuple-element.131) | copy-start | bytes 3145732
  12.8 435.8 %collective-permute-start = (bf16[2,8,512,1,128]{4,2,1,0,3:T(8,128)(2,1)}, bf16[2,8,512,1,128]{4,2,1,0,3:T(8,128)(2,1)}, u32[]{:S(2)}, u32[]{:S(2)}) collective-permute-start(bf16[2,8,512,1,128]{4,2,1,0,3:T(8,128)(2,1)} %pad_maximum_fusion), channel_id=1, source_target_pairs={{0,8},{8,16},{16,24},{24,32},{32,40},{40,48},{48,56},{56,64},{64,7... | collective-permute-start | bytes 6291464 | tf_op jit(solution)/shard_map/ppermute | solution.py:12
  17.9 430.7 %collective-permute-start.1 = (bf16[2,8,512,1,128]{4,2,1,0,3:T(8,128)(2,1)}, bf16[2,8,512,1,128]{4,2,1,0,3:T(8,128)(2,1)}, u32[]{:S(2)}, u32[]{:S(2)}) collective-permute-start(bf16[2,8,512,1,128]{4,2,1,0,3:T(8,128)(2,1)} %pad_maximum_fusion), channel_id=1, source_target_pairs={{8,0},{16,8},{24,16},{32,24},{40,32},{48,40},{56,48},{64,56},{72,6... | collective-permute-start | bytes 6291464 | tf_op jit(solution)/shard_map/ppermute | solution.py:12
  121.3 8.6 %copy-start.2 = (bf16[2,2048,1,128]{3,1,0,2:T(8,128)(2,1)S(1)}, bf16[2,2048,1,128]{3,1,0,2:T(8,128)(2,1)}, u32[]{:S(2)}) copy-start(bf16[2,2048,1,128]{3,1,0,2:T(8,128)(2,1)} %get-tuple-element.215) | copy-start | bytes 3145732 | tf_op jit(solution)/shard_map/while
  146.5 8.6 %copy-start.2 = (bf16[2,2048,1,128]{3,1,0,2:T(8,128)(2,1)S(1)}, bf16[2,2048,1,128]{3,1,0,2:T(8,128)(2,1)}, u32[]{:S(2)}) copy-start(bf16[2,2048,1,128]{3,1,0,2:T(8,128)(2,1)} %get-tuple-element.215) | copy-start | bytes 3145732 | tf_op jit(solution)/shard_map/while
  162.7 72.0 %copy-start.5 = (bf16[8,1,128]{2,0,1:T(8,128)(2,1)S(1)}, bf16[8,1,128]{2,0,1:T(8,128)(2,1)}, u32[]{:S(2)}) copy-start(bf16[8,1,128]{2,0,1:T(8,128)(2,1)} %param.16) | copy-start | bytes 6148
  162.7 72.6 %copy-start.7 = (u32[256]{0:T(256)S(1)}, u32[256]{0:T(256)}, u32[]{:S(2)}) copy-start(u32[256]{0:T(256)} %constant.68) | copy-start | bytes 3076
  162.7 211.4 %copy-start.6 = (s32[8]{0:T(128)S(1)}, s32[8]{0:T(128)}, u32[]{:S(2)}) copy-start(s32[8]{0:T(128)} %param.19) | copy-start | bytes 100
  162.7 211.4 %copy-start.4 = (bf16[8,1,128]{2,0,1:T(8,128)(2,1)S(1)}, bf16[8,1,128]{2,0,1:T(8,128)(2,1)}, u32[]{:S(2)}) copy-start(bf16[8,1,128]{2,0,1:T(8,128)(2,1)} %param.17) | copy-start | bytes 6148
  230.4 218.2 %copy-start.1 = (bf16[1,8,512,1,128]{4,2,1,0,3:T(8,128)(2,1)S(1)}, bf16[1,8,512,1,128]{4,2,1,0,3:T(8,128)(2,1)}, u32[]{:S(2)}) copy-start(bf16[1,8,512,1,128]{4,2,1,0,3:T(8,128)(2,1)} %copy-done) | copy-start | bytes 3145732
Sparse Core Ops, SparseCore 0:
  233.1 213.2 reduce-scatter.2
where the time goes:
time: 470 us; the launch traced here: 466 us
  blocking collectives  296 us (63%)
  waiting for transfers between devices  72.3 us (15%)
  matrix products  36.6 us (8%)
  other arithmetic  31.5 us (7%)
  between operations  14.9 us (3%)
  local copies, waits for them, and re-layouts  8.45 us (2%)
  starting transfers between devices  6.98 us (1%)
    unnamed x1, blocking collectives  137 us
    all_gather x1, blocking collectives, on_device(): all_particles_view = lax.all_gather(queries, 'seq', axis=0, tiled=True)  92.3 us
    reduce_scatter x1, waiting for transfers between devices, on_device(): lax.psum_scatter(weighted * factor[..., None], 'seq', scatter_dimension=0...  72.2 us
    pmax x1, blocking collectives, on_device(): global_max = lax.pmax(maxima, 'seq')  66.2 us
    dot_general x2, matrix products, visit(): jnp.einsum('vmfu,zmu->vmfz', all_particles_view, block_of_keys, preferred...  18.2 us
    reduce_sum x2, other arithmetic, visit(): block_sum = jnp.sum(weights, axis=3)  17.1 us
    dot_general x2, matrix products, visit(): jnp.einsum('yvho,ovq->yvhq', weights.astype(jnp.bfloat16), value_block, p...  15 us
  transfers between devices with their start and end apart: 3, of which 1 were waited for; matrix products, arithmetic and copies ran while one was open for 13% of the time, Pallas kernels for 0%

commit v1 on v0

v1 whole, which is shorter than its diff:
```python
import functools
import math

import jax
import jax.numpy as jnp
from jax import lax
from jax.experimental import pallas as pl
from jax.experimental.pallas import tpu as pltpu
from jax.sharding import PartitionSpec as P

F32, BF16, I16, I32 = jnp.float32, jnp.bfloat16, jnp.int16, jnp.int32
MESH = pl.DeviceIdType.MESH
HD = 128
GROUP = 8
PART = 8
HALO = 4
ROWS = PART * GROUP
NX, NZ = 4, 8
TILE = 256
TILES = NX * NZ * ROWS // TILE
CHUNK = 512
LOG2E = math.log2(math.e)
SCALE = LOG2E / math.sqrt(HD)
CODE = 32000.0


def column(rows, j):
    return rows[:, j : j + 1]


def turned(parts):
    sub = lax.broadcasted_iota(I32, (16, HD), 0)
    top = jnp.zeros((16, HD), F32)
    for j, part in enumerate(parts):
        top = jnp.where(sub == j, part, top)
    return jnp.concatenate([top, jnp.zeros((HD - 16, HD), F32)], axis=0).T


def coded(values):
    largest = jnp.maximum(jnp.max(jnp.abs(values), axis=1, keepdims=True), 1e-30)
    codes = jnp.round(values * (CODE / largest)).astype(I32).astype(I16)
    return codes, largest


def attention_kernel(
    q_hbm,
    k_hbm,
    v_hbm,
    sk_hbm,
    sv_hbm,
    nk_ref,
    nv_ref,
    len_ref,
    att_ref,
    bk_hbm,
    bv_hbm,
    ak_hbm,
    av_hbm,
    bnew_ref,
    anew_ref,
    blen_ref,
    alen_ref,
    q_all,
    k_all,
    vx,
    sk,
    sv,
    new_own,
    len_own,
    s0,
    s1,
    m0,
    m1,
    acc,
    suf_o,
    suf_m,
    suf_l,
    own_o,
    own_st,
    xs_code,
    xs_st,
    xr_code,
    xr_st,
    zs_code,
    zs_st,
    zr_code,
    zr_st,
    out_rows,
    local_sem,
    agz_s,
    agz_r,
    agx_s,
    agx_r,
    rsx_s,
    rsx_r,
    rsz_s,
    rsz_r,
    halo_s,
    halo_r,
    small_s,
    small_r,
):
    me = lax.axis_index("seq")
    x, z = me // NZ, me % NZ
    owners = NX * NZ
    above, below = (me + 1) % owners, (me + owners - 1) % owners

    def z_peer(k):
        return x * NZ + (z + k) % NZ

    def x_peer(j):
        return ((x + j + j // 2 - 2 * (j // 3)) % NX) * NZ + z

    def back(j):
        return 3 - j + 3 * (j // 3)

    def remote(src, dst, send, recv, device):
        return pltpu.make_async_remote_copy(
            src, dst, send, recv, device_id={"seq": device}, device_id_type=MESH
        )

    partners = [z_peer(k) for k in range(1, NZ)] + [x_peer(j) for j in (1, 2, 3)] + [above, below]
    barrier = pltpu.get_barrier_semaphore()
    for p in partners:
        pl.semaphore_signal(barrier, inc=1, device_id={"seq": p}, device_id_type=MESH)

    def z_rows(zz):
        return pl.multiple_of(zz * ROWS + (zz // 4) * (TILES - 2) * TILE, ROWS)

    own_rows = pl.ds(z_rows(z), ROWS)
    locals_ = [
        pltpu.make_async_copy(q_hbm, q_all.at[own_rows], local_sem.at[0]),
        pltpu.make_async_copy(sk_hbm, sk, local_sem.at[1]),
        pltpu.make_async_copy(sv_hbm, sv, local_sem.at[2]),
        pltpu.make_async_copy(k_hbm, k_all, local_sem.at[3]),
        pltpu.make_async_copy(v_hbm, vx.at[:, pl.ds(0, HD)], local_sem.at[4]),
    ]
    for c in locals_:
        c.start()

    new_own[...] = jnp.concatenate(
        [nk_ref[...].astype(F32), nv_ref[...].astype(F32)], axis=0
    ).astype(BF16)
    sub = lax.broadcasted_iota(I32, (PART, HD), 0)
    lens = jnp.zeros((PART, HD), I32)
    for p in range(PART):
        lens = jnp.where(sub == p, len_ref[p], lens)
    len_own[...] = lens
    pl.semaphore_wait(barrier, len(partners))

    agz = [
        remote(q_hbm, q_all.at[own_rows], agz_s.at[k - 1], agz_r.at[NZ - 1 - k], z_peer(k))
        for k in range(1, NZ)
    ]
    agz_in = [
        remote(
            q_hbm,
            q_all.at[pl.ds(z_rows((z + k) % NZ), ROWS)],
            agz_s.at[k - 1],
            agz_r.at[k - 1],
            z_peer(k),
        )
        for k in range(1, NZ)
    ]
    for c in agz:
        c.start()

    small = [
        remote(new_own, bnew_ref, small_s.at[0], small_r.at[0], above),
        remote(new_own, anew_ref, small_s.at[1], small_r.at[1], below),
        remote(len_own, blen_ref, small_s.at[2], small_r.at[2], above),
        remote(len_own, alen_ref, small_s.at[3], small_r.at[3], below),
    ]
    for c in small:
        c.start()

    def halo(j):
        low, high = pl.ds(j, 1), pl.ds(j + PART - HALO, 1)
        return [
            remote(sk_hbm.at[high], bk_hbm.at[low], halo_s.at[j, 0], halo_r.at[j, 0], above),
            remote(sk_hbm.at[low], ak_hbm.at[low], halo_s.at[j, 1], halo_r.at[j, 1], below),
            remote(sv_hbm.at[high], bv_hbm.at[low], halo_s.at[j, 2], halo_r.at[j, 2], above),
            remote(sv_hbm.at[low], av_hbm.at[low], halo_s.at[j, 3], halo_r.at[j, 3], below),
        ]

    for c in halo(0):
        c.start()

    for c in locals_[:3]:
        c.wait()
    q_own = q_all[own_rows, :]
    q_own32 = q_own.astype(F32)
    nk32, nv32 = nk_ref[...].astype(F32), nv_ref[...].astype(F32)
    slot = lax.broadcasted_iota(I32, (GROUP, sk.shape[1]), 1)
    for p in range(PART):
        mine = slice(p * GROUP, (p + 1) * GROUP)
        s = lax.dot_general(q_own, sk[p], (((1,), (1,)), ((), ())), preferred_element_type=F32)
        s = s[mine] * SCALE
        new = jnp.sum(q_own32[mine] * nk32[p : p + 1], axis=1, keepdims=True) * SCALE
        live = slot < len_ref[p]
        top = jnp.maximum(jnp.max(jnp.where(live, s, -1e30), axis=1, keepdims=True), new)
        w = jnp.where(live, jnp.exp2(s - top), 0.0)
        nw = jnp.exp2(new - top)
        wide = jnp.concatenate([w, jnp.zeros_like(w)], axis=0).astype(BF16)
        o = jnp.dot(wide, sv[p], preferred_element_type=F32)[:GROUP]
        suf_o[mine, :] = o + nw.astype(BF16).astype(F32) * nv32[p : p + 1]
        suf_m[mine, :] = jnp.broadcast_to(top, (GROUP, HD))
        suf_l[mine, :] = jnp.broadcast_to(jnp.sum(w, axis=1, keepdims=True) + nw, (GROUP, HD))
    vx[:, HD:] = jnp.ones((vx.shape[0], HD), BF16)
    for c in locals_[3:]:
        c.wait()

    for c in agz_in:
        c.wait_recv()

    def agx(n, slot_there):
        half = n % 2
        src = q_all.at[pl.ds(half * (TILES - 1) * TILE, TILE)]
        dst = q_all.at[pl.ds(pl.multiple_of((1 + 2 * (slot_there - 1) + half) * TILE, TILE), TILE)]
        return src, dst

    def agx_out(n):
        j = n // 2 + 1
        src, dst = agx(n, back(j))
        return remote(src, dst, agx_s.at[n], agx_r.at[2 * (back(j) - 1) + n % 2], x_peer(j))

    def agx_in(n):
        j = n // 2 + 1
        src, dst = agx(n, j)
        return remote(src, dst, agx_s.at[n], agx_r.at[n], x_peer(j))

    for n in range(6):
        agx_out(n).start()

    def scores(t, keys):
        q = q_all[pl.ds(pl.multiple_of(t * TILE, TILE), TILE), :]
        return lax.dot_general(
            q, k_all[keys, :], (((1,), (1,)), ((), ())), preferred_element_type=F32
        )

    n_chunks = k_all.shape[0] // CHUNK

    def step(t, s_next, m_next, s_now, m_now):
        most = None
        for c in range(n_chunks):
            keys = slice(c * CHUNK, (c + 1) * CHUNK)
            if s_next is not None:
                s = scores(t + 1, keys)
                s_next[:, keys] = s
                for g in range(CHUNK // HD):
                    part = s[:, g * HD : (g + 1) * HD]
                    most = part if most is None else jnp.maximum(most, part)
            if s_now is not None:
                top = m_now[...]
                weights = [
                    jnp.exp2(s_now[:, lo : lo + HD] * SCALE - top).astype(BF16)
                    for lo in range(c * CHUNK, (c + 1) * CHUNK, HD)
                ]
                d = jnp.dot(
                    jnp.concatenate(weights, axis=1), vx[keys, :], preferred_element_type=F32
                )
                if c == 0:
                    acc[...] = d
                else:
                    acc[...] += d
        if s_next is not None:
            m_next[...] = jnp.broadcast_to(
                jnp.max(most, axis=1, keepdims=True) * SCALE, m_next.shape
            )

    lane = lax.broadcasted_iota(I32, (TILE, HD), 1)

    def normalised(m_now):
        total = acc[:, HD:]
        return acc[:, :HD] / total, m_now[...] + jnp.log(total) * LOG2E

    def put_stats(ref, lse, largest):
        both = jnp.where(lane == 0, lse, jnp.broadcast_to(largest, lse.shape))
        for g in range(TILE // HD):
            ref[g * 8 : (g + 1) * 8, :] = both[g * HD : (g + 1) * HD].T[:8]

    def rsx_copies(n, slot_there):
        i = 2 * (slot_there - 1) + n % 2
        j = n // 2 + 1
        return [
            remote(xs_code.at[n], xr_code.at[i], rsx_s.at[n, 0], rsx_r.at[i, 0], x_peer(j)),
            remote(xs_st.at[n], xr_st.at[i], rsx_s.at[n, 1], rsx_r.at[i, 1], x_peer(j)),
        ]

    def finish_peer(t, m_now):
        n = t - 1
        o, lse = normalised(m_now)
        codes, largest = coded(o)
        xs_code[n] = codes
        put_stats(xs_st.at[n], lse, largest)
        for c in rsx_copies(n, back(n // 2 + 1)):
            c.start()

    def finish_own(half, m_now):
        o, lse = normalised(m_now)
        own_o[half * TILE : (half + 1) * TILE, :] = o
        put_stats(own_st.at[half], lse, jnp.ones((TILE, 1), F32))

    step(-1, s0, m0, None, None)
    agx_in(0).wait_recv()
    step(0, s1, m1, s0, m0)
    finish_own(0, m0)

    def pair(i, _):
        t = 2 * i + 1
        for c in halo(i + 1):
            c.start()
        agx_in(t).wait_recv()
        step(t, s0, m0, s1, m1)
        finish_peer(t, m1)
        agx_in(t + 1).wait_recv()
        step(t + 1, s1, m1, s0, m0)
        finish_peer(t + 1, m0)
        return 0

    lax.fori_loop(0, 2, pair, 0)
    agx_in(5).wait_recv()
    step(5, s0, m0, s1, m1)
    finish_peer(5, m1)
    step(6, s1, m1, s0, m0)
    finish_peer(6, m0)
    step(7, None, None, s1, m1)
    finish_own(1, m1)

    def sum_x(half):
        for j in (1, 2, 3):
            n = 2 * (j - 1) + half
            for c in rsx_copies(n, j):
                c.wait_recv()
        for g in range(TILE // HD):
            rows = slice(g * HD, (g + 1) * HD)
            lse = [own_st[half, g * 8 : g * 8 + 1, :]]
            for j in range(3):
                lse.append(xr_st[2 * j + half, g * 8 : g * 8 + 1, :])
            top = functools.reduce(jnp.maximum, lse)
            w = [jnp.exp2(v - top) for v in lse]
            total = functools.reduce(jnp.add, w)
            factors = [w[0] / total]
            for j in range(3):
                largest = xr_st[2 * j + half, g * 8 + 1 : g * 8 + 2, :]
                factors.append(w[j + 1] / total * (largest * (1.0 / CODE)))
            cols = turned(factors)
            at = half * TILE + g * HD
            o = own_o[at : at + HD, :] * column(cols, 0)
            for j in range(3):
                codes = xr_code[2 * j + half, rows, :].astype(I32).astype(F32)
                o = o + codes * column(cols, j + 1)
            codes, largest = coded(o)
            zs_code[at : at + HD, :] = codes
            st = jnp.broadcast_to(largest, (HD, HD)).T[:8]
            sub8 = lax.broadcasted_iota(I32, (8, HD), 0)
            zs_st[at // HD] = jnp.where(sub8 == 0, top + jnp.log(total) * LOG2E, st)

    def z_copies(k, to_there):
        there = (z + k) % NZ
        src = there if to_there else z
        slot_ = z if to_there else there
        i = NZ - 1 - k if to_there else k - 1
        return [
            remote(
                zs_code.at[pl.ds(pl.multiple_of(there * ROWS, ROWS), ROWS)],
                zr_code.at[slot_],
                rsz_s.at[k - 1, 0],
                rsz_r.at[i, 0],
                z_peer(k),
            ),
            remote(zs_st.at[there // 2], zr_st.at[slot_], rsz_s.at[k - 1, 1], rsz_r.at[i, 1], z_peer(k)),
        ]

    sum_x(0)
    sum_x(1)
    for k in range(1, NZ):
        for c in z_copies(k, True):
            c.start()
    for c in halo(3):
        c.start()
    zr_code[z] = zs_code[pl.ds(pl.multiple_of(z * ROWS, ROWS), ROWS), :]
    zr_st[z] = zs_st[z // 2]
    for k in range(1, NZ):
        for c in z_copies(k, False):
            c.wait_recv()

    odd = z % 2 == 1
    lse, largest = [], []
    for i in range(NZ):
        st = zr_st[i]
        st = jnp.where(odd, pltpu.roll(st, HD // 2, 1), st)
        lse.append(st[0:1])
        largest.append(st[1:2])
    top = functools.reduce(jnp.maximum, lse)
    w = [jnp.exp2(v - top) for v in lse]
    total = functools.reduce(jnp.add, w)
    cols = turned([a * (b * (1.0 / CODE)) for a, b in zip(w, largest)] + [total, top])[:ROWS]
    o = jnp.zeros((ROWS, HD), F32)
    for i in range(NZ):
        o = o + zr_code[i].astype(I32).astype(F32) * column(cols, i)
    prompt_sum, prompt_max = column(cols, NZ), column(cols, NZ + 1)
    suffix_max = suf_m[...]
    both = jnp.maximum(prompt_max, suffix_max)
    first, second = jnp.exp2(prompt_max - both), jnp.exp2(suffix_max - both)
    denom = prompt_sum * first + suf_l[...] * second
    out_rows[...] = (o * first + suf_o[...] * second) / denom
    for h in range(GROUP):
        att_ref[:, h * HD : (h + 1) * HD] = out_rows[pl.ds(h, PART, stride=GROUP), :].astype(BF16)

    for c in agz:
        c.wait_send()
    for n in range(6):
        agx_out(n).wait_send()
        for c in rsx_copies(n, back(n // 2 + 1)):
            c.wait_send()
    for k in range(1, NZ):
        for c in z_copies(k, True):
            c.wait_send()
    for c in small:
        c.wait()
    for j in range(HALO):
        for c in halo(j):
            c.wait()


def resample_kernel(
    anc_ref,
    len_ref,
    blen_ref,
    alen_ref,
    nk_ref,
    nv_ref,
    bnew_ref,
    anew_ref,
    att_in,
    sk_hbm,
    sv_hbm,
    bk_hbm,
    bv_hbm,
    ak_hbm,
    av_hbm,
    att_ref,
    nk_hbm,
    nv_hbm,
    buf,
    fresh,
    in_sem,
    out_sem,
):
    first = lax.axis_index("seq") * PART
    slots = sk_hbm.shape[1]
    fresh[0:8, :] = nk_ref[...].astype(F32)
    fresh[8:16, :] = nv_ref[...].astype(F32)
    fresh[16:32, :] = bnew_ref[...].astype(F32)
    fresh[32:48, :] = anew_ref[...].astype(F32)
    att_ref[...] = att_in[...]

    def fetch(q, where, kind):
        local = anc_ref[q] - first
        own, low, high = (sk_hbm, bk_hbm, ak_hbm) if kind == 0 else (sv_hbm, bv_hbm, av_hbm)
        dst, sem = buf.at[2 * q + kind], in_sem.at[2 * q + kind]

        @pl.when(local < 0)
        def _():
            pltpu.make_async_copy(low.at[jnp.maximum(local + HALO, 0)], dst, sem).start()

        @pl.when(local >= PART)
        def _():
            pltpu.make_async_copy(
                high.at[jnp.minimum(jnp.maximum(local - PART, 0), HALO - 1)], dst, sem
            ).start()

        @pl.when(jnp.logical_and(local >= 0, local < PART))
        def _():
            pltpu.make_async_copy(
                own.at[jnp.minimum(jnp.maximum(local, 0), PART - 1)], dst, sem
            ).start()

    for q in range(PART):
        for kind in range(2):
            fetch(q, 0, kind)

    row = lax.broadcasted_iota(I32, (slots, HD), 0)
    for q in range(PART):
        local = anc_ref[q] - first
        is_low, is_high = local < 0, local >= PART
        at = jnp.where(is_low, local + PART, jnp.where(is_high, local - PART, local))
        at = jnp.minimum(jnp.maximum(at, 0), PART - 1)
        length = jnp.where(
            is_low, blen_ref[at, 0], jnp.where(is_high, alen_ref[at, 0], len_ref[at])
        )
        base = jnp.where(is_low, 16, jnp.where(is_high, 32, 0)) + at
        for kind in range(2):
            i = 2 * q + kind
            out = nk_hbm if kind == 0 else nv_hbm
            pltpu.make_async_copy(sk_hbm.at[0], buf.at[i], in_sem.at[i]).wait()
            fresh_row = fresh[pl.ds(base + kind * PART, 1), :]
            kept = jnp.where(row < length, buf[i].astype(F32), 0.0)
            buf[i] = jnp.where(row == length, fresh_row, kept).astype(BF16)
            pltpu.make_async_copy(buf.at[i], out.at[q], out_sem.at[i]).start()
    for q in range(PART):
        for kind in range(2):
            i = 2 * q + kind
            out = nk_hbm if kind == 0 else nv_hbm
            pltpu.make_async_copy(buf.at[i], out.at[q], out_sem.at[i]).wait()


def on_device(
    queries,
    prompt_keys,
    prompt_values,
    suffix_keys,
    suffix_values,
    new_keys,
    new_values,
    suffix_len,
    ancestors,
):
    slots, keys = suffix_keys.shape[1], prompt_keys.shape[0]
    q = queries.reshape(ROWS, HD)
    k, v = prompt_keys.reshape(keys, HD), prompt_values.reshape(keys, HD)
    sk, sv = suffix_keys.reshape(PART, slots, HD), suffix_values.reshape(PART, slots, HD)
    nk, nv = new_keys.reshape(PART, HD), new_values.reshape(PART, HD)
    any_, vmem, smem = (
        pl.BlockSpec(memory_space=pl.ANY),
        pl.BlockSpec(memory_space=pltpu.VMEM),
        pl.BlockSpec(memory_space=pltpu.SMEM),
    )
    shape = jax.ShapeDtypeStruct
    side = shape((HALO, slots, HD), BF16)
    dma = pltpu.SemaphoreType.DMA
    att, bk, bv, ak, av, bnew, anew, blen, alen = pl.pallas_call(
        attention_kernel,
        out_shape=(
            shape((PART, GROUP * HD), BF16),
            side,
            side,
            side,
            side,
            shape((2 * PART, HD), BF16),
            shape((2 * PART, HD), BF16),
            shape((PART, HD), I32),
            shape((PART, HD), I32),
        ),
        in_specs=[any_] * 5 + [vmem, vmem, smem],
        out_specs=(vmem, any_, any_, any_, any_, vmem, vmem, vmem, vmem),
        scratch_shapes=[
            pltpu.VMEM((TILES * TILE, HD), BF16),
            pltpu.VMEM((keys, HD), BF16),
            pltpu.VMEM((keys, 2 * HD), BF16),
            pltpu.VMEM((PART, slots, HD), BF16),
            pltpu.VMEM((PART, slots, HD), BF16),
            pltpu.VMEM((2 * PART, HD), BF16),
            pltpu.VMEM((PART, HD), I32),
            pltpu.VMEM((TILE, keys), F32),
            pltpu.VMEM((TILE, keys), F32),
            pltpu.VMEM((TILE, HD), F32),
            pltpu.VMEM((TILE, HD), F32),
            pltpu.VMEM((TILE, 2 * HD), F32),
            pltpu.VMEM((ROWS, HD), F32),
            pltpu.VMEM((ROWS, HD), F32),
            pltpu.VMEM((ROWS, HD), F32),
            pltpu.VMEM((2 * TILE, HD), F32),
            pltpu.VMEM((2, TILE // 16, HD), F32),
            pltpu.VMEM((6, TILE, HD), I16),
            pltpu.VMEM((6, TILE // 16, HD), F32),
            pltpu.VMEM((6, TILE, HD), I16),
            pltpu.VMEM((6, TILE // 16, HD), F32),
            pltpu.VMEM((2 * TILE, HD), I16),
            pltpu.VMEM((4, 8, HD), F32),
            pltpu.VMEM((NZ, ROWS, HD), I16),
            pltpu.VMEM((NZ, 8, HD), F32),
            pltpu.VMEM((ROWS, HD), F32),
            dma((5,)),
            dma((NZ - 1,)),
            dma((NZ - 1,)),
            dma((6,)),
            dma((6,)),
            dma((6, 2)),
            dma((6, 2)),
            dma((NZ - 1, 2)),
            dma((NZ - 1, 2)),
            dma((HALO, 4)),
            dma((HALO, 4)),
            dma((4,)),
            dma((4,)),
        ],
        compiler_params=pltpu.CompilerParams(
            collective_id=0, has_side_effects=True, vmem_limit_bytes=40 * 2**20
        ),
        name="attention",
    )(q, k, v, sk, sv, nk, nv, suffix_len)
    attended, next_keys, next_values = pl.pallas_call(
        resample_kernel,
        out_shape=(
            shape((PART, GROUP * HD), BF16),
            shape((PART, slots, HD), BF16),
            shape((PART, slots, HD), BF16),
        ),
        in_specs=[smem] * 4 + [vmem] * 5 + [any_] * 6,
        out_specs=(vmem, any_, any_),
        scratch_shapes=[
            pltpu.VMEM((2 * PART, slots, HD), BF16),
            pltpu.VMEM((6 * PART, HD), F32),
            dma((2 * PART,)),
            dma((2 * PART,)),
        ],
        compiler_params=pltpu.CompilerParams(vmem_limit_bytes=32 * 2**20),
        name="resample",
    )(ancestors, suffix_len, blen, alen, nk, nv, bnew, anew, att, sk, sv, bk, bv, ak, av)
    return (
        attended,
        next_keys.reshape(suffix_keys.shape),
        next_values.reshape(suffix_values.shape),
    )


def solution(mesh):
    in_specs = (
        P("seq", "head", None),
        P("seq", "head", None),
        P("seq", "head", None),
        P("seq", None, "head", None),
        P("seq", None, "head", None),
        P("seq", "head", None),
        P("seq", "head", None),
        P("seq"),
        P("seq"),
    )
    out_specs = (P("seq", "head"), P("seq", None, "head", None), P("seq", None, "head", None))
    return jax.shard_map(
        on_device, mesh=mesh, in_specs=in_specs, out_specs=out_specs, check_vma=False
    )
```

time: 470 us -> 77.4 us (0.16)
  the two profiles are of different devices: /device:TPU:120 before, /device:TPU:8 now
where the time goes in v1:
time: 77.4 us; the launch traced here: 77 us
  Pallas kernels  69.4 us (90%)
  local copies, waits for them, and re-layouts  6.94 us (9%)
    pallas_call x1, Pallas kernels, on_device(): pl.pallas_call(attention_kernel, out_shape=(shape((PART, GROUP * HD), BF1...  63 us
    unnamed x18, local copies, waits for them, and re-layouts  6.94 us
    pallas_call x1, Pallas kernels, on_device(): pl.pallas_call(resample_kernel, out_shape=(shape((PART, GROUP * HD), BF16...  6.41 us

profile of v1, /device:TPU:8, one launch (start us, length us, event | category | flops | bytes accessed | tf_op | source)
XLA Modules:
  0.0 77.0 jit_solution(10148115042012446201)
XLA Ops:
  0.6 0.0 copy-start.6
  0.6 0.0 copy-start.5
  0.7 0.0 copy-start.7
  0.7 0.7 copy-done.6
  1.3 0.0 copy-done.5
  1.3 0.0 copy-done.7
  1.3 0.0 copy-start
  1.3 1.2 %copy-done = bf16[8,512,1,128]{3,1,2,0:T(8,128)(2,1)S(1)} copy-done((bf16[8,512,1,128]{3,1,2,0:T(8,128)(2,1)S(1)}, bf16[8,512,1,128]{3,1,2,0:T(8,128)(2,1)}, u32[]{:S(2)}) %copy-start) | copy-done | bytes 1048600
  2.6 0.0 copy-start.1
  2.6 1.2 %copy-done.1 = bf16[8,512,1,128]{3,1,2,0:T(8,128)(2,1)S(1)} copy-done((bf16[8,512,1,128]{3,1,2,0:T(8,128)(2,1)S(1)}, bf16[8,512,1,128]{3,1,2,0:T(8,128)(2,1)}, u32[]{:S(2)}) %copy-start.1) | copy-done | bytes 1048600
  3.8 0.0 copy-start.2
  3.8 1.2 %copy-done.2 = bf16[4096,1,128]{2,0,1:T(8,128)(2,1)S(1)} copy-done((bf16[4096,1,128]{2,0,1:T(8,128)(2,1)S(1)}, bf16[4096,1,128]{2,0,1:T(8,128)(2,1)}, u32[]{:S(2)}) %copy-start.2) | copy-done | bytes 1048600
  5.0 0.0 copy-start.3
  5.0 1.2 %copy-done.3 = bf16[4096,1,128]{2,0,1:T(8,128)(2,1)S(1)} copy-done((bf16[4096,1,128]{2,0,1:T(8,128)(2,1)S(1)}, bf16[4096,1,128]{2,0,1:T(8,128)(2,1)}, u32[]{:S(2)}) %copy-start.3) | copy-done | bytes 1048600
  6.2 0.0 copy-start.4
  6.2 0.7 copy-done.4
  7.0 63.0 %attention.1 = (bf16[8,1024]{1,0:T(8,128)(2,1)S(1)}, bf16[4,512,128]{2,1,0:T(8,128)(2,1)S(1)}, bf16[4,512,128]{2,1,0:T(8,128)(2,1)S(1)}, bf16[4,512,128]{2,1,0:T...) custom-call(bf16[64,128]{1,0:T(8,128)(2,1)S(1)} %bitcast.19, ...), custom_call_target="tpu_custom_call" | custom-call | tf_op jit(solution)/shard_map/attention/pallas_call | solution.py:533
  70.0 0.0 copy-start.8
  70.0 0.6 copy-done.8
  70.6 6.4 %resample.1 = (bf16[8,1024]{1,0:T(8,128)(2,1)}, bf16[8,512,128]{2,1,0:T(8,128)(2,1)}, bf16[8,512,128]{2,1,0:T(8,128)(2,1)}) custom-call(s32[8]{0:T(128)S(1)} %copy-done.8, s32[8]{0:T(128)S(1)} %copy-done.7, s32[8,128]{1,0:T(8,128)S(1)} %get-tuple-element.15.blen_ref, s32[8,128]{1,0:T(8,128)S(1)} %get-tuple-element.16.alen_ref, bf16[8,128]{1,0:T(8,128)(2,1)S(1)} %bitcast.21, ...), custom_call_target="tpu_custom_call" | custom-call | tf_op jit(solution)/shard_map/resample/pallas_call | solution.py:594
Async XLA Ops:
  0.6 0.7 copy-start.6
  0.6 0.7 copy-start.5
  0.7 0.7 copy-start.7
  1.3 1.2 %copy-start = (bf16[8,512,1,128]{3,1,2,0:T(8,128)(2,1)S(1)}, bf16[8,512,1,128]{3,1,2,0:T(8,128)(2,1)}, u32[]{:S(2)}) copy-start(bf16[8,512,1,128]{3,1,2,0:T(8,128)(2,1)} %param.12) | copy-start | bytes 3145732
  2.6 1.2 %copy-start.1 = (bf16[8,512,1,128]{3,1,2,0:T(8,128)(2,1)S(1)}, bf16[8,512,1,128]{3,1,2,0:T(8,128)(2,1)}, u32[]{:S(2)}) copy-start(bf16[8,512,1,128]{3,1,2,0:T(8,128)(2,1)} %param.13) | copy-start | bytes 3145732
  3.8 1.2 %copy-start.2 = (bf16[4096,1,128]{2,0,1:T(8,128)(2,1)S(1)}, bf16[4096,1,128]{2,0,1:T(8,128)(2,1)}, u32[]{:S(2)}) copy-start(bf16[4096,1,128]{2,0,1:T(8,128)(2,1)} %param.10) | copy-start | bytes 3145732
  5.0 1.2 %copy-start.3 = (bf16[4096,1,128]{2,0,1:T(8,128)(2,1)S(1)}, bf16[4096,1,128]{2,0,1:T(8,128)(2,1)}, u32[]{:S(2)}) copy-start(bf16[4096,1,128]{2,0,1:T(8,128)(2,1)} %param.11) | copy-start | bytes 3145732
  6.2 0.7 copy-start.4
  70.0 0.7 copy-start.8

commit v2 on v1

v2 whole, which is shorter than its diff:
```python
import functools
import math

import jax
import jax.numpy as jnp
from jax import lax
from jax.experimental import pallas as pl
from jax.experimental.pallas import tpu as pltpu
from jax.sharding import PartitionSpec as P

F32, BF16, I16, I32 = jnp.float32, jnp.bfloat16, jnp.int16, jnp.int32
MESH = pl.DeviceIdType.MESH
HD = 128
GROUP = 8
PART = 8
HALO = 4
ROWS = PART * GROUP
NX, NZ = 4, 8
TILE = 256
TILES = NX * NZ * ROWS // TILE
CHUNK = 512
LOG2E = math.log2(math.e)
SCALE = LOG2E / math.sqrt(HD)
OFFSETS = (0, 1, 7, 2, 6, 3, 5, 4)
NEGATIVE = (0, 2, 1, 4, 3, 6, 5, 7)
CUT = 32
BUDGET = 42
PACKETS = 3
PACKET_AT = (-1, 1, 2)
VMEM_LIMIT = 60 * 2**20
CODE = 32000.0


def column(rows, j):
    return rows[:, j : j + 1]


def turned(parts):
    sub = lax.broadcasted_iota(I32, (16, HD), 0)
    top = jnp.zeros((16, HD), F32)
    for j, part in enumerate(parts):
        top = jnp.where(sub == j, part, top)
    return jnp.concatenate([top, jnp.zeros((HD - 16, HD), F32)], axis=0).T


def coded(values):
    largest = jnp.maximum(jnp.max(jnp.abs(values), axis=1, keepdims=True), 1e-30)
    codes = jnp.round(values * (CODE / largest)).astype(I32).astype(I16)
    return codes, largest


def attention_kernel(
    q_hbm,
    k_hbm,
    v_hbm,
    sk_hbm,
    sv_hbm,
    nk_hbm,
    nv_hbm,
    len_hbm,
    anc_hbm,
    att_ref,
    wk_hbm,
    wv_hbm,
    lowk_hbm,
    lowv_hbm,
    highk_hbm,
    highv_hbm,
    low_info,
    high_info,
    need_ref,
    q_all,
    k_all,
    vx,
    sk,
    sv,
    nk_ref,
    nv_ref,
    fresh,
    len_ref,
    anc_ref,
    info,
    low_at,
    high_at,
    to_above_k,
    to_above_v,
    to_below_k,
    to_below_v,
    s0,
    s1,
    m0,
    m1,
    acc,
    suf_o,
    suf_m,
    suf_l,
    own_o,
    own_st,
    xs_code,
    xs_st,
    xr_code,
    xr_st,
    zs_code,
    zs_st,
    zr_code,
    zr_st,
    out_rows,
    local_sem,
    win_sem,
    agz_s,
    agz_r,
    agx_s,
    agx_r,
    rsx_s,
    rsx_r,
    rsz_s,
    rsz_r,
    info_sem,
    info_s,
    info_r,
    halo_s,
    halo_r,
):
    me = lax.axis_index("seq")
    x, z = me // NZ, me % NZ
    owners = NX * NZ
    above, below = (me + 1) % owners, (me + owners - 1) % owners

    def z_peer(pos):
        return x * NZ + (z + OFFSETS[pos]) % NZ

    def x_peer(j):
        return ((x + j + j // 2 - 2 * (j // 3)) % NX) * NZ + z

    def back(j):
        return 3 - j + 3 * (j // 3)

    def remote(src, dst, send, recv, device):
        return pltpu.make_async_remote_copy(
            src, dst, send, recv, device_id={"seq": device}, device_id_type=MESH
        )

    partners = [z_peer(p) for p in range(1, NZ)] + [x_peer(j) for j in (1, 2, 3)] + [above, below]
    barrier = pltpu.get_barrier_semaphore()
    for p in partners:
        pl.semaphore_signal(barrier, inc=1, device_id={"seq": p}, device_id_type=MESH)

    def tile_of(j, half):
        return j if half == 0 else 4 + j % 3

    def own_rows(pos, count=1):
        return pl.ds((TILES - 1) * TILE * (pos // 4) + (pos % 4) * ROWS, count * ROWS)

    locals_ = [
        pltpu.make_async_copy(q_hbm, q_all.at[own_rows(0)], local_sem.at[0]),
        pltpu.make_async_copy(nk_hbm, nk_ref, local_sem.at[1]),
        pltpu.make_async_copy(nv_hbm, nv_ref, local_sem.at[2]),
        pltpu.make_async_copy(len_hbm, len_ref, local_sem.at[3]),
        pltpu.make_async_copy(sk_hbm, sk, local_sem.at[4]),
        pltpu.make_async_copy(sv_hbm, sv, local_sem.at[5]),
        pltpu.make_async_copy(k_hbm, k_all, local_sem.at[6]),
        pltpu.make_async_copy(v_hbm, vx.at[:, pl.ds(0, HD)], local_sem.at[7]),
        pltpu.make_async_copy(anc_hbm, anc_ref, local_sem.at[8]),
    ]
    for c in locals_:
        c.start()
    vx[:, HD:] = jnp.ones((vx.shape[0], HD), BF16)

    locals_[3].wait()
    locals_[8].wait()
    sub = lax.broadcasted_iota(I32, (PART, HD), 0)
    lane8 = lax.broadcasted_iota(I32, (PART, HD), 1)
    table = jnp.zeros((PART, HD), I32)
    for p in range(PART):
        table = jnp.where(sub == p, jnp.where(lane8 == 0, len_ref[p], anc_ref[p]), table)
    info[...] = table
    pl.semaphore_wait(barrier, len(partners))
    infos = [
        remote(info, low_info, info_s.at[0], info_r.at[0], above),
        remote(info, high_info, info_s.at[1], info_r.at[1], below),
    ]
    for c in infos:
        c.start()

    def agz_out(pos):
        return remote(
            q_hbm,
            q_all.at[own_rows(NEGATIVE[pos])],
            agz_s.at[pos - 1],
            agz_r.at[NEGATIVE[pos] - 1],
            z_peer(pos),
        )

    def agz_in(pos):
        return remote(
            q_hbm, q_all.at[own_rows(pos)], agz_s.at[pos - 1], agz_r.at[pos - 1], z_peer(pos)
        )

    parts = ((0, 1), (1, 3), (4, 4))

    def agx(part, j, slot_there):
        pos, count = parts[part]
        start = tile_of(slot_there, pos // 4) * TILE + (pos % 4) * ROWS
        src = q_hbm if part == 0 else q_all.at[own_rows(pos, count)]
        return src, q_all.at[pl.ds(start, count * ROWS)]

    def agx_out(part, j):
        src, dst = agx(part, j, back(j))
        return remote(src, dst, agx_s.at[part, j - 1], agx_r.at[part, back(j) - 1], x_peer(j))

    def agx_in(part, j):
        src, dst = agx(part, j, j)
        return remote(src, dst, agx_s.at[part, j - 1], agx_r.at[part, j - 1], x_peer(j))

    for pos in range(1, NZ):
        agz_out(pos).start()
    for j in (1, 2, 3):
        agx_out(0, j).start()

    for i in (0, 1, 2, 4, 5):
        locals_[i].wait()
    fresh[0:PART, :] = nk_ref[...].astype(F32)
    fresh[PART : 2 * PART, :] = nv_ref[...].astype(F32)
    pieces = sk.shape[0] // PART
    slots = pieces * CUT
    row = lax.broadcasted_iota(I32, (pieces, CUT, HD), 0) * CUT + lax.broadcasted_iota(
        I32, (pieces, CUT, HD), 1
    )

    def update(p):
        mine = slice(p * pieces, (p + 1) * pieces)
        for kind, cache in ((0, sk), (1, sv)):
            new = fresh[kind * PART + p : kind * PART + p + 1, :].reshape(1, 1, HD)
            kept = jnp.where(row < len_ref[p], cache[mine].astype(F32), 0.0)
            cache[mine] = jnp.where(row == len_ref[p], new, kept).astype(BF16)

    first = me * PART

    def starts(ancestors, lengths, base):
        at = [0]
        for j in range(HALO):
            wanted = functools.reduce(
                jnp.maximum, [jnp.where(ancestors(q) == base + j, 1, 0) for q in range(PART)]
            )
            at.append(at[-1] + wanted * (lengths(j) // CUT + 1))
        return at

    def pack(at, base, to_k, to_v):
        def body(i, _):
            j = sum(jnp.where(i >= at[n], 1, 0) for n in (1, 2, 3))
            begin = functools.reduce(
                jnp.maximum, [jnp.where(i >= at[n], at[n], 0) for n in (1, 2, 3)]
            )
            piece = (base + j) * pieces + jnp.minimum(i - begin, pieces - 1)
            to_k[i] = sk[piece]
            to_v[i] = sv[piece]
            return 0

        lax.fori_loop(0, BUDGET, body, 0, unroll=3)

    def packet(n):
        rows = pl.ds(n * (BUDGET // PACKETS), BUDGET // PACKETS)
        return [
            remote(src.at[rows], dst.at[rows], halo_s.at[n, i], halo_r.at[n, i], device)
            for i, (src, dst, device) in enumerate(
                (
                    (to_above_k, lowk_hbm, above),
                    (to_below_k, highk_hbm, below),
                    (to_above_v, lowv_hbm, above),
                    (to_below_v, highv_hbm, below),
                )
            )
        ]

    for pos in (1, 2, 3):
        agz_in(pos).wait_recv()
    for j in (1, 2, 3):
        agx_out(1, j).start()
    for p in range(PART):
        update(p)
    window = [
        pltpu.make_async_copy(sk, wk_hbm, win_sem.at[0]),
        pltpu.make_async_copy(sv, wv_hbm, win_sem.at[1]),
    ]
    for c in window:
        c.start()
    for c in infos:
        c.wait_recv()
    tables = [
        pltpu.make_async_copy(low_info, low_at, info_sem.at[0]),
        pltpu.make_async_copy(high_info, high_at, info_sem.at[1]),
    ]
    for c in tables:
        c.start()
    for c in tables:
        c.wait()
    pack(
        starts(lambda q: high_at[q, 1], lambda j: len_ref[PART - HALO + j], first + PART - HALO),
        PART - HALO,
        to_above_k,
        to_above_v,
    )
    pack(starts(lambda q: low_at[q, 1], lambda j: len_ref[j], first), 0, to_below_k, to_below_v)
    need = jnp.maximum(
        starts(lambda q: anc_ref[q], lambda j: low_at[PART - HALO + j, 0], first - HALO)[-1],
        starts(lambda q: anc_ref[q], lambda j: high_at[j, 0], first + PART)[-1],
    ).astype(F32)
    for n in range(PACKETS):
        if PACKET_AT[n] < 0:
            for c in packet(n):
                c.start()
    for pos in (4, 5, 6, 7):
        agz_in(pos).wait_recv()
    for j in (1, 2, 3):
        agx_out(2, j).start()
    for c in locals_[6:8]:
        c.wait()

    def scores(t, keys):
        q = q_all[pl.ds(pl.multiple_of(t * TILE, TILE), TILE), :]
        return lax.dot_general(
            q, k_all[keys, :], (((1,), (1,)), ((), ())), preferred_element_type=F32
        )

    n_chunks = k_all.shape[0] // CHUNK

    def step(t, s_next, m_next, s_now, m_now):
        most = None
        for c in range(n_chunks):
            keys = slice(c * CHUNK, (c + 1) * CHUNK)
            if s_next is not None:
                s = scores(t + 1, keys)
                s_next[:, keys] = s
                for g in range(CHUNK // HD):
                    part = s[:, g * HD : (g + 1) * HD]
                    most = part if most is None else jnp.maximum(most, part)
            if s_now is not None:
                top = m_now[...]
                weights = [
                    jnp.exp2(s_now[:, lo : lo + HD] * SCALE - top).astype(BF16)
                    for lo in range(c * CHUNK, (c + 1) * CHUNK, HD)
                ]
                d = jnp.dot(
                    jnp.concatenate(weights, axis=1), vx[keys, :], preferred_element_type=F32
                )
                if c == 0:
                    acc[...] = d
                else:
                    acc[...] += d
        if s_next is not None:
            m_next[...] = jnp.broadcast_to(
                jnp.max(most, axis=1, keepdims=True) * SCALE, m_next.shape
            )

    lane = lax.broadcasted_iota(I32, (TILE, HD), 1)

    def normalised(m_now):
        total = acc[:, HD:]
        return acc[:, :HD] / total, m_now[...] + jnp.log(total) * LOG2E

    def put_stats(ref, lse, largest):
        both = jnp.where(lane == 0, lse, jnp.broadcast_to(largest, lse.shape))
        for g in range(TILE // HD):
            st = both[g * HD : (g + 1) * HD].T[:8]
            ref[g * 8 : (g + 1) * 8, :] = jnp.where(sub == 2, need, st)

    def slot_of(n):
        return n + 1 - n // 3 * (4 - 3 * ((5 - n) // 2))

    def rsx_copies(n, i, j):
        return [
            remote(xs_code.at[n], xr_code.at[i], rsx_s.at[n, 0], rsx_r.at[i, 0], x_peer(j)),
            remote(xs_st.at[n], xr_st.at[i], rsx_s.at[n, 1], rsx_r.at[i, 1], x_peer(j)),
        ]

    def rsx_out(n):
        j = slot_of(n)
        half = n // 3
        return rsx_copies(n, 2 * (back(j) - 1) + half, j)

    def rsx_in(j, half):
        i = 2 * (j - 1) + half
        return rsx_copies(i, i, j)

    def finish_peer(t, m_now):
        n = t - 1
        o, lse = normalised(m_now)
        codes, largest = coded(o)
        xs_code[n] = codes
        put_stats(xs_st.at[n], lse, largest)
        for c in rsx_out(n):
            c.start()

    def finish_own(half, m_now):
        o, lse = normalised(m_now)
        own_o[half * TILE : (half + 1) * TILE, :] = o
        put_stats(own_st.at[half], lse, jnp.ones((TILE, 1), F32))

    def wait_tile(t):
        for n in range(6):
            j, half = (1, 2, 3, 3, 1, 2)[n], n // 3

            @pl.when(t == n + 1)
            def _():
                for part in (0, 1) if half == 0 else (2,):
                    agx_in(part, j).wait_recv()

    step(-1, s0, m0, None, None)

    def pair(i, _):
        t = 2 * i
        for n in range(PACKETS):

            @pl.when(i == PACKET_AT[n])
            def _():
                for c in packet(n):
                    c.start()

        wait_tile(t + 1)
        step(t, s1, m1, s0, m0)

        @pl.when(t == 0)
        def _():
            finish_own(0, m0)

        @pl.when(t > 0)
        def _():
            finish_peer(t, m0)

        wait_tile(t + 2)
        step(t + 1, s0, m0, s1, m1)
        finish_peer(t + 1, m1)
        return 0

    lax.fori_loop(0, 3, pair, 0)

    def sum_x(half):
        for j in (1, 2, 3):
            for c in rsx_in(j, half):
                c.wait_recv()
        for g in range(TILE // HD):
            rows = slice(g * HD, (g + 1) * HD)
            lse = [own_st[half, g * 8 : g * 8 + 1, :]]
            for j in range(3):
                lse.append(xr_st[2 * j + half, g * 8 : g * 8 + 1, :])
            top = functools.reduce(jnp.maximum, lse)
            w = [jnp.exp2(v - top) for v in lse]
            total = functools.reduce(jnp.add, w)
            factors = [w[0] / total]
            for j in range(3):
                largest = xr_st[2 * j + half, g * 8 + 1 : g * 8 + 2, :]
                factors.append(w[j + 1] / total * (largest * (1.0 / CODE)))
            cols = turned(factors)
            at = half * TILE + g * HD
            o = own_o[at : at + HD, :] * column(cols, 0)
            for j in range(3):
                codes = xr_code[2 * j + half, rows, :].astype(I32).astype(F32)
                o = o + codes * column(cols, j + 1)
            codes, largest = coded(o)
            zs_code[at : at + HD, :] = codes
            st = jnp.broadcast_to(largest, (HD, HD)).T[:8]
            sub8 = lax.broadcasted_iota(I32, (8, HD), 0)
            most = own_st[half, 2:3, :]
            for j in range(3):
                most = jnp.maximum(most, xr_st[2 * j + half, 2:3, :])
            st = jnp.where(sub8 == 2, most, st)
            zs_st[at // HD] = jnp.where(sub8 == 0, top + jnp.log(total) * LOG2E, st)

    def z_copies(pos, i):
        return [
            remote(
                zs_code.at[pl.ds(pos * ROWS, ROWS)],
                zr_code.at[i],
                rsz_s.at[pos - 1, 0],
                rsz_r.at[i - 1, 0],
                z_peer(pos),
            ),
            remote(
                zs_st.at[pos // 2], zr_st.at[i], rsz_s.at[pos - 1, 1], rsz_r.at[i - 1, 1], z_peer(pos)
            ),
        ]

    def z_out(pos):
        return z_copies(pos, NEGATIVE[pos])

    sum_x(0)
    for pos in (1, 2, 3):
        for c in z_out(pos):
            c.start()
    step(6, s1, m1, s0, m0)
    finish_peer(6, m0)
    step(7, None, None, s1, m1)
    finish_own(1, m1)
    sum_x(1)
    for pos in (4, 5, 6, 7):
        for c in z_out(pos):
            c.start()
    for n in range(PACKETS):
        if PACKET_AT[n] > 2:
            for c in packet(n):
                c.start()

    q_own = q_all[own_rows(0), :]
    q_own32 = q_own.astype(F32)
    slot = lax.broadcasted_iota(I32, (GROUP, slots), 1)
    for p in range(PART):
        mine = slice(p * GROUP, (p + 1) * GROUP)
        some = slice(p * pieces, (p + 1) * pieces)
        own_k, own_v = sk[some].reshape(slots, HD), sv[some].reshape(slots, HD)
        s = lax.dot_general(q_own, own_k, (((1,), (1,)), ((), ())), preferred_element_type=F32)
        s = s[mine] * SCALE
        new = jnp.sum(q_own32[mine] * fresh[p : p + 1, :], axis=1, keepdims=True) * SCALE
        live = slot < len_ref[p]
        top = jnp.maximum(jnp.max(jnp.where(live, s, -1e30), axis=1, keepdims=True), new)
        w = jnp.where(live, jnp.exp2(s - top), 0.0)
        nw = jnp.exp2(new - top)
        wide = jnp.concatenate([w, jnp.zeros_like(w)], axis=0).astype(BF16)
        o = jnp.dot(wide, own_v, preferred_element_type=F32)[:GROUP]
        suf_o[mine, :] = o + nw.astype(BF16).astype(F32) * fresh[PART + p : PART + p + 1, :]
        suf_m[mine, :] = jnp.broadcast_to(top, (GROUP, HD))
        suf_l[mine, :] = jnp.broadcast_to(jnp.sum(w, axis=1, keepdims=True) + nw, (GROUP, HD))

    zr_code[0] = zs_code[0:ROWS, :]
    zr_st[0] = zs_st[0]
    for pos in range(1, NZ):
        for c in z_copies(pos, pos):
            c.wait_recv()

    lse, largest = [], []
    need_ref[...] = functools.reduce(jnp.maximum, [zr_st[i] for i in range(NZ)])
    for i in range(NZ):
        st = zr_st[i]
        if NEGATIVE[i] % 2 == 1:
            st = pltpu.roll(st, HD // 2, 1)
        lse.append(st[0:1])
        largest.append(st[1:2])
    top = functools.reduce(jnp.maximum, lse)
    w = [jnp.exp2(v - top) for v in lse]
    total = functools.reduce(jnp.add, w)
    cols = turned([a * (b * (1.0 / CODE)) for a, b in zip(w, largest)] + [total, top])[:ROWS]
    o = jnp.zeros((ROWS, HD), F32)
    for i in range(NZ):
        o = o + zr_code[i].astype(I32).astype(F32) * column(cols, i)
    prompt_sum, prompt_max = column(cols, NZ), column(cols, NZ + 1)
    suffix_max = suf_m[...]
    both = jnp.maximum(prompt_max, suffix_max)
    first, second = jnp.exp2(prompt_max - both), jnp.exp2(suffix_max - both)
    denom = prompt_sum * first + suf_l[...] * second
    out_rows[...] = (o * first + suf_o[...] * second) / denom
    for h in range(GROUP):
        att_ref[:, h * HD : (h + 1) * HD] = out_rows[pl.ds(h, PART, stride=GROUP), :].astype(BF16)

    for pos in range(1, NZ):
        agz_out(pos).wait_send()
        for c in z_out(pos):
            c.wait_send()
    for j in (1, 2, 3):
        for part in range(3):
            agx_out(part, j).wait_send()
    for n in range(6):
        for c in rsx_out(n):
            c.wait_send()
    for c in window:
        c.wait()
    for c in infos:
        c.wait_send()
    for n in range(PACKETS):
        for c in packet(n):
            c.wait()


def halo_kernel(k_hbm, v_hbm, lowk, lowv, highk, highv, send, recv):
    me = lax.axis_index("seq")
    owners = NX * NZ
    above, below = (me + 1) % owners, (me + owners - 1) % owners
    pieces = k_hbm.shape[0] // PART
    barrier = pltpu.get_barrier_semaphore()
    for p in (above, below):
        pl.semaphore_signal(barrier, inc=1, device_id={"seq": p}, device_id_type=MESH)
    pl.semaphore_wait(barrier, 2)
    copies = [
        pltpu.make_async_remote_copy(
            src.at[pl.ds(at * pieces, HALO * pieces)],
            dst,
            send.at[i],
            recv.at[i],
            device_id={"seq": device},
            device_id_type=MESH,
        )
        for i, (src, at, dst, device) in enumerate(
            (
                (k_hbm, PART - HALO, lowk, above),
                (v_hbm, PART - HALO, lowv, above),
                (k_hbm, 0, highk, below),
                (v_hbm, 0, highv, below),
            )
        )
    ]
    for c in copies:
        c.start()
    for c in copies:
        c.wait()


def resample_kernel(
    packed,
    anc_ref,
    low_ref,
    high_ref,
    att_in,
    k_hbm,
    v_hbm,
    lowk,
    lowv,
    highk,
    highv,
    att_ref,
    nk_hbm,
    nv_hbm,
    buf,
    att_buf,
    in_sem,
    out_sem,
):
    first = lax.axis_index("seq") * PART
    slots = k_hbm.shape[0] * CUT // PART
    pieces = slots // CUT
    att = [
        pltpu.make_async_copy(att_in, att_buf, in_sem.at[2 * PART]),
        pltpu.make_async_copy(att_buf, att_ref, out_sem.at[2 * PART]),
    ]
    att[0].start()

    def places(base, lengths):
        row, out = 0, []
        for j in range(HALO):
            live = lengths(j) // CUT + 1
            out.append((row if packed else j * pieces, live))
            wanted = functools.reduce(
                jnp.maximum, [jnp.where(anc_ref[q] == base + j, 1, 0) for q in range(PART)]
            )
            row = row + wanted * live
        return out

    low = places(first - HALO, lambda j: low_ref[PART - HALO + j, 0])
    high = places(first + PART, lambda j: high_ref[j, 0])

    def pick(entries, j, which):
        value = entries[0][which]
        for n in range(1, HALO):
            value = jnp.where(j == n, entries[n][which], value)
        return value

    at = [anc_ref[q] - first for q in range(PART)]

    def fetch(q):
        local = at[q]

        def start(k, v):
            pltpu.make_async_copy(k, buf.at[2 * q], in_sem.at[2 * q]).start()
            pltpu.make_async_copy(v, buf.at[2 * q + 1], in_sem.at[2 * q + 1]).start()

        def side(entries, j, k, v):
            limit = k.shape[0] - pieces
            rows = pl.ds(jnp.minimum(jnp.maximum(pick(entries, j, 0), 0), limit), pieces)
            start(k.at[rows], v.at[rows])

        @pl.when(local < 0)
        def _():
            side(low, local + HALO, lowk, lowv)

        @pl.when(local >= PART)
        def _():
            side(high, local - PART, highk, highv)

        @pl.when(jnp.logical_and(local >= 0, local < PART))
        def _():
            own = jnp.minimum(jnp.maximum(local, 0), PART - 1)
            rows = pl.ds(own * pieces, pieces)
            start(k_hbm.at[rows], v_hbm.at[rows])

    for q in range(PART):
        fetch(q)
    row = lax.broadcasted_iota(I32, (pieces, CUT, HD), 0)
    for q in range(PART):
        local = at[q]
        for kind, out in ((0, nk_hbm), (1, nv_hbm)):
            i = 2 * q + kind
            pltpu.make_async_copy(k_hbm.at[pl.ds(0, pieces)], buf.at[i], in_sem.at[i]).wait()
            if packed:

                @pl.when(jnp.logical_or(local < 0, local >= PART))
                def _():
                    live = jnp.where(
                        local < 0, pick(low, local + HALO, 1), pick(high, local - PART, 1)
                    )
                    buf[i] = jnp.where(row < live, buf[i].astype(F32), 0.0).astype(BF16)

            pltpu.make_async_copy(buf.at[i], out.at[pl.ds(q * pieces, pieces)], out_sem.at[i]).start()
    att[0].wait()
    att[1].start()
    for q in range(PART):
        for kind, out in ((0, nk_hbm), (1, nv_hbm)):
            i = 2 * q + kind
            pltpu.make_async_copy(buf.at[i], out.at[pl.ds(q * pieces, pieces)], out_sem.at[i]).wait()
    att[1].wait()


def on_device(
    queries,
    prompt_keys,
    prompt_values,
    suffix_keys,
    suffix_values,
    new_keys,
    new_values,
    suffix_len,
    ancestors,
):
    slots, keys = suffix_keys.shape[1], prompt_keys.shape[0]
    q = queries.reshape(ROWS, HD)
    k, v = prompt_keys.reshape(keys, HD), prompt_values.reshape(keys, HD)
    sk = suffix_keys.reshape(PART * slots // CUT, CUT, HD)
    sv = suffix_values.reshape(PART * slots // CUT, CUT, HD)
    nk, nv = new_keys.reshape(PART, HD), new_values.reshape(PART, HD)
    hbm, vmem, smem = (
        pl.BlockSpec(memory_space=pltpu.HBM),
        pl.BlockSpec(memory_space=pltpu.VMEM),
        pl.BlockSpec(memory_space=pltpu.SMEM),
    )
    shape = jax.ShapeDtypeStruct
    window = shape((PART * slots // CUT, CUT, HD), BF16)
    side = shape((BUDGET + slots // CUT, CUT, HD), BF16)
    info = shape((PART, HD), I32)
    dma = pltpu.SemaphoreType.DMA
    att, wk, wv, lowk, lowv, highk, highv, low_info, high_info, need = pl.pallas_call(
        attention_kernel,
        out_shape=(
            shape((PART, GROUP * HD), BF16),
            window,
            window,
            side,
            side,
            side,
            side,
            info,
            info,
            shape((PART, HD), F32),
        ),
        in_specs=[hbm] * 9,
        out_specs=(vmem, hbm, hbm, hbm, hbm, hbm, hbm, vmem, vmem, vmem),
        scratch_shapes=[
            pltpu.VMEM((TILES * TILE, HD), BF16),
            pltpu.VMEM((keys, HD), BF16),
            pltpu.VMEM((keys, 2 * HD), BF16),
            pltpu.VMEM((PART * slots // CUT, CUT, HD), BF16),
            pltpu.VMEM((PART * slots // CUT, CUT, HD), BF16),
            pltpu.VMEM((PART, HD), BF16),
            pltpu.VMEM((PART, HD), BF16),
            pltpu.VMEM((2 * PART, HD), F32),
            pltpu.SMEM((PART,), I32),
            pltpu.SMEM((PART,), I32),
            pltpu.VMEM((PART, HD), I32),
            pltpu.SMEM((PART, HD), I32),
            pltpu.SMEM((PART, HD), I32),
            pltpu.VMEM((BUDGET, CUT, HD), BF16),
            pltpu.VMEM((BUDGET, CUT, HD), BF16),
            pltpu.VMEM((BUDGET, CUT, HD), BF16),
            pltpu.VMEM((BUDGET, CUT, HD), BF16),
            pltpu.VMEM((TILE, keys), F32),
            pltpu.VMEM((TILE, keys), F32),
            pltpu.VMEM((TILE, HD), F32),
            pltpu.VMEM((TILE, HD), F32),
            pltpu.VMEM((TILE, 2 * HD), F32),
            pltpu.VMEM((ROWS, HD), F32),
            pltpu.VMEM((ROWS, HD), F32),
            pltpu.VMEM((ROWS, HD), F32),
            pltpu.VMEM((2 * TILE, HD), F32),
            pltpu.VMEM((2, TILE // 16, HD), F32),
            pltpu.VMEM((6, TILE, HD), I16),
            pltpu.VMEM((6, TILE // 16, HD), F32),
            pltpu.VMEM((6, TILE, HD), I16),
            pltpu.VMEM((6, TILE // 16, HD), F32),
            pltpu.VMEM((2 * TILE, HD), I16),
            pltpu.VMEM((4, 8, HD), F32),
            pltpu.VMEM((NZ, ROWS, HD), I16),
            pltpu.VMEM((NZ, 8, HD), F32),
            pltpu.VMEM((ROWS, HD), F32),
            dma((9,)),
            dma((2,)),
            dma((NZ - 1,)),
            dma((NZ - 1,)),
            dma((3, 3)),
            dma((3, 3)),
            dma((6, 2)),
            dma((6, 2)),
            dma((NZ - 1, 2)),
            dma((NZ - 1, 2)),
            dma((2,)),
            dma((2,)),
            dma((2,)),
            dma((PACKETS, 4)),
            dma((PACKETS, 4)),
        ],
        compiler_params=pltpu.CompilerParams(
            collective_id=0, has_side_effects=True, vmem_limit_bytes=VMEM_LIMIT
        ),
        name="attention",
    )(q, k, v, sk, sv, nk, nv, suffix_len, ancestors)

    def resample(packed, *operands):
        return pl.pallas_call(
            functools.partial(resample_kernel, packed),
            out_shape=(
                shape((PART, GROUP * HD), BF16),
                window,
                window,
            ),
            in_specs=[smem, smem, smem] + [hbm] * 7,
            out_specs=(hbm, hbm, hbm),
            scratch_shapes=[
                pltpu.VMEM((2 * PART, slots // CUT, CUT, HD), BF16),
                pltpu.VMEM((PART, GROUP * HD), BF16),
                dma((2 * PART + 1,)),
                dma((2 * PART + 1,)),
            ],
            compiler_params=pltpu.CompilerParams(vmem_limit_bytes=VMEM_LIMIT),
            name="resample",
        )(*operands)

    def whole(anc, low_info, high_info, att, wk, wv, *_):
        full = shape((HALO * slots // CUT, CUT, HD), BF16)
        sides = pl.pallas_call(
            halo_kernel,
            out_shape=(full,) * 4,
            in_specs=[hbm] * 2,
            out_specs=(hbm,) * 4,
            scratch_shapes=[dma((4,)), dma((4,))],
            compiler_params=pltpu.CompilerParams(
                collective_id=1, has_side_effects=True, vmem_limit_bytes=VMEM_LIMIT
            ),
            name="halo",
        )(wk, wv)
        return resample(False, anc, low_info, high_info, att, wk, wv, *sides)

    attended, next_keys, next_values = lax.cond(
        need[2, 0] <= BUDGET,
        functools.partial(resample, True),
        whole,
        ancestors,
        low_info,
        high_info,
        att,
        wk,
        wv,
        lowk,
        lowv,
        highk,
        highv,
    )
    return (
        attended,
        next_keys.reshape(suffix_keys.shape),
        next_values.reshape(suffix_values.shape),
    )


def solution(mesh):
    in_specs = (
        P("seq", "head", None),
        P("seq", "head", None),
        P("seq", "head", None),
        P("seq", None, "head", None),
        P("seq", None, "head", None),
        P("seq", "head", None),
        P("seq", "head", None),
        P("seq"),
        P("seq"),
    )
    out_specs = (P("seq", "head"), P("seq", None, "head", None), P("seq", None, "head", None))
    return jax.shard_map(
        on_device, mesh=mesh, in_specs=in_specs, out_specs=out_specs, check_vma=False
    )
```

time: 77.4 us -> 61.9 us (0.80)
  the two profiles are of different devices: /device:TPU:8 before, /device:TPU:120 now
where the time goes in v2:
time: 61.9 us; the launch traced here: 61.8 us
  Pallas kernels  58.6 us (95%)
  local copies, waits for them, and re-layouts  1.84 us (3%)
  between operations  1.3 us (2%)
    pallas_call x1, Pallas kernels, on_device(): pl.pallas_call(attention_kernel, out_shape=(shape((PART, GROUP * HD), BF1...  53.3 us
    pallas_call x1, Pallas kernels, resample(): pl.pallas_call(functools.partial(resample_kernel, packed), out_shape=(sha...  5.31 us

profile of v2, /device:TPU:120, one launch (start us, length us, event | category | flops | bytes accessed | tf_op | source)
XLA Modules:
  0.0 61.8 jit_solution(13469219365289702429)
XLA Ops:
  0.6 0.0 copy-start
  0.6 0.6 %copy-done = s32[8]{0:T(128)S(1)} copy-done((s32[8]{0:T(128)S(1)}, s32[8]{0:T(128)}, u32[]{:S(2)}) %copy-start) | copy-done | bytes 56
  1.3 53.3 %attention.1 = (bf16[8,1024]{1,0:T(8,128)(2,1)S(1)}, bf16[128,32,128]{2,1,0:T(8,128)(2,1)S(1)}, bf16[128,32,128]{2,1,0:T(8,128)(2,1)S(1)}, bf16[58,32,128]{2,1,0...) custom-call(bf16[64,128]{1,0:T(8,128)(2,1)} %bitcast.14, ...), custom_call_target="tpu_custom_call" | custom-call | tf_op jit(solution)/shard_map/attention/pallas_call | solution.py:736
  54.6 1.2 %slice.3 = f32[1,1]{1,0:T(1,128)} slice(f32[8,128]{1,0:T(8,128)} %get-tuple-element.79), slice={[2:3], [0:1]} | slice | bytes 8 | tf_op jit(solution)/shard_map/slice | solution.py:847
  56.4 5.3 %conditional.1 = ((bf16[8,1024]{1,0:T(8,128)(2,1)}, bf16[128,32,128]{2,1,0:T(8,128)(2,1)}, bf16[128,32,128]{2,1,0:T(8,128)(2,1)})) conditional(s32[]{:T(128)} %bitcast.7, (bf16[128,32,128]{2,1,0:T(8,128)(2,1)S(1)}, bf16[128,32,128]{2,1,0:T(8,128)(2,1)S(1)}, s32[8]{0:T(128)S(1)}, s32[8,128]{1,0:T(8,128)S(1)}, s32[8,128]{1,0:T(8,128)S(1)}, ...), branch_computations={%region_0.0_spmd, %region_1.0_spmd} | conditional | bytes 8 | solution.py:846
  56.4 5.3 %resample.3 = (bf16[8,1024]{1,0:T(8,128)(2,1)}, bf16[128,32,128]{2,1,0:T(8,128)(2,1)}, bf16[128,32,128]{2,1,0:T(8,128)(2,1)}) custom-call(s32[8]{0:T(128)S(1)} %get-tuple-element.53.anc_ref, s32[8,128]{1,0:T(8,128)S(1)} %get-tuple-element.54.low_ref, s32[8,128]{1,0:T(8,128)S(1)} %get-tuple-element.55.high_ref, bf16[8,1024]{1,0:T(8,128)(2,1)S(1)} %get-tuple-element.56.att_in, ...), custom_call_target="tpu_custom_call" | custom-call | tf_op jit(solution)/shard_map/cond/branch_1_fun/resample/pallas_call | solution.py:812
Async XLA Ops:
  0.6 0.7 %copy-start = (s32[8]{0:T(128)S(1)}, s32[8]{0:T(128)}, u32[]{:S(2)}) copy-start(s32[8]{0:T(128)} %anc_hbm.1) | copy-start | bytes 100

commit v3 on v2

--- a/solution.py
+++ b/solution.py
@@ -24,9 +24,11 @@
 OFFSETS = (0, 1, 7, 2, 6, 3, 5, 4)
 NEGATIVE = (0, 2, 1, 4, 3, 6, 5, 7)
 CUT = 32
-BUDGET = 42
-PACKETS = 3
-PACKET_AT = (-1, 1, 2)
+BUDGET = 44
+CROSS = 34
+PACKETS = 4
+PACKET_AT = (-1, 0, 1, 2)
+CROSS_AT = (1, 0, 2)
 VMEM_LIMIT = 60 * 2**20
 CODE = 32000.0
 
@@ -66,9 +68,8 @@
     lowv_hbm,
     highk_hbm,
     highv_hbm,
-    low_info,
-    high_info,
-    need_ref,
+    plan_ref,
+    fits_ref,
     q_all,
     k_all,
     vx,
@@ -80,12 +81,16 @@
     len_ref,
     anc_ref,
     info,
+    low_info,
+    high_info,
     low_at,
     high_at,
     to_above_k,
     to_above_v,
     to_below_k,
     to_below_v,
+    relay_k,
+    relay_v,
     s0,
     s1,
     m0,
@@ -120,6 +125,8 @@
     info_r,
     halo_s,
     halo_r,
+    cross_s,
+    cross_r,
 ):
     me = lax.axis_index("seq")
     x, z = me // NZ, me % NZ
@@ -256,21 +263,83 @@
             to_v[i] = sv[piece]
             return 0
 
-        lax.fori_loop(0, BUDGET, body, 0, unroll=3)
-
-    def packet(n):
+        lax.fori_loop(0, BUDGET, body, 0, unroll=4)
+
+    to_above, to_below = (to_above_k, to_above_v), (to_below_k, to_below_v)
+    low, high = (lowk_hbm, lowv_hbm), (highk_hbm, highv_hbm)
+    at_top, at_bottom = z == NZ - 1, z == 0
+
+    def packet(n, up):
         rows = pl.ds(n * (BUDGET // PACKETS), BUDGET // PACKETS)
+        src, dst, device = (to_above, low, above) if up else (to_below, high, below)
+        i = 0 if up else 2
         return [
-            remote(src.at[rows], dst.at[rows], halo_s.at[n, i], halo_r.at[n, i], device)
-            for i, (src, dst, device) in enumerate(
-                (
-                    (to_above_k, lowk_hbm, above),
-                    (to_below_k, highk_hbm, below),
-                    (to_above_v, lowv_hbm, above),
-                    (to_below_v, highv_hbm, below),
-                )
+            remote(
+                src[kind].at[rows],
+                dst[kind].at[rows],
+                halo_s.at[n, i + kind],
+                halo_r.at[n, i + kind],
+                device,
             )
+            for kind in range(2)
         ]
+
+    def cross(stage, up):
+        src, dst, device = (to_above, low, above) if up else (to_below, high, below)
+        near, far = pl.ds(0, CROSS // 2), pl.ds(CROSS // 2, CROSS // 2)
+        relay = (relay_k, relay_v)
+        along = 1 if up else 2
+        out = []
+        for kind in range(2):
+            if stage == 0:
+                ends = src[kind].at[near], dst[kind].at[near], device
+            elif stage == 1:
+                ends = src[kind].at[far], relay[kind], x_peer(along)
+            else:
+                ends = relay[kind], dst[kind].at[far], z_peer(along)
+            a, b, there = ends
+            out.append(remote(a, b, cross_s.at[stage, kind], cross_r.at[stage, kind], there))
+        return out
+
+    def send_halo(when):
+        for n in range(PACKETS):
+            for up, edge in ((True, at_top), (False, at_bottom)):
+
+                @pl.when(jnp.logical_and(when == PACKET_AT[n], jnp.logical_not(edge)))
+                def _():
+                    for c in packet(n, up):
+                        c.start()
+
+        for stage in range(3):
+            for up, edge in ((True, at_top), (False, at_bottom)):
+
+                @pl.when(jnp.logical_and(when == CROSS_AT[stage], edge))
+                def _():
+                    if stage == 2:
+                        for c in cross(1, up):
+                            c.wait_recv()
+                    for c in cross(stage, up):
+                        c.start()
+
+    def finish_halo():
+        for up, edge in ((True, at_top), (False, at_bottom)):
+
+            @pl.when(jnp.logical_not(edge))
+            def _():
+                for n in range(PACKETS):
+                    for c in packet(n, up):
+                        c.wait_send()
+                    for c in packet(n, not up):
+                        c.wait_recv()
+
+            @pl.when(edge)
+            def _():
+                for stage in range(3):
+                    for c in cross(stage, up):
+                        c.wait_send()
+                for stage in (0, 2):
+                    for c in cross(stage, not up):
+                        c.wait_recv()
 
     for pos in (1, 2, 3):
         agz_in(pos).wait_recv()
@@ -301,14 +370,30 @@
         to_above_v,
     )
     pack(starts(lambda q: low_at[q, 1], lambda j: len_ref[j], first), 0, to_below_k, to_below_v)
+    extra = BUDGET - CROSS
+    low_row = starts(lambda q: anc_ref[q], lambda j: low_at[PART - HALO + j, 0], first - HALO)
+    high_row = starts(lambda q: anc_ref[q], lambda j: high_at[j, 0], first + PART)
     need = jnp.maximum(
-        starts(lambda q: anc_ref[q], lambda j: low_at[PART - HALO + j, 0], first - HALO)[-1],
-        starts(lambda q: anc_ref[q], lambda j: high_at[j, 0], first + PART)[-1],
+        low_row[-1] + jnp.where(at_bottom, extra, 0), high_row[-1] + jnp.where(at_top, extra, 0)
     ).astype(F32)
-    for n in range(PACKETS):
-        if PACKET_AT[n] < 0:
-            for c in packet(n):
-                c.start()
+
+    for q in range(PART):
+        local = anc_ref[q] - first
+        is_low, is_high = local < 0, local >= PART
+        place = jnp.where(is_low, local + HALO, jnp.where(is_high, local - PART, local))
+        begin, live = local * pieces, pieces
+        for j in range(HALO):
+            chosen = jnp.logical_and(is_low, place == j)
+            begin = jnp.where(chosen, low_row[j], begin)
+            live = jnp.where(chosen, low_at[PART - HALO + j, 0] // CUT + 1, live)
+            chosen = jnp.logical_and(is_high, place == j)
+            begin = jnp.where(chosen, high_row[j], begin)
+            live = jnp.where(chosen, high_at[j, 0] // CUT + 1, live)
+        plan_ref[q] = jnp.where(is_low, 1, jnp.where(is_high, 2, 0))
+        plan_ref[PART + q] = place
+        plan_ref[2 * PART + q] = begin
+        plan_ref[3 * PART + q] = live
+    send_halo(-1)
     for pos in (4, 5, 6, 7):
         agz_in(pos).wait_recv()
     for j in (1, 2, 3):
@@ -409,13 +494,7 @@
 
     def pair(i, _):
         t = 2 * i
-        for n in range(PACKETS):
-
-            @pl.when(i == PACKET_AT[n])
-            def _():
-                for c in packet(n):
-                    c.start()
-
+        send_halo(i)
         wait_tile(t + 1)
         step(t, s1, m1, s0, m0)
 
@@ -495,10 +574,7 @@
     for pos in (4, 5, 6, 7):
         for c in z_out(pos):
             c.start()
-    for n in range(PACKETS):
-        if PACKET_AT[n] > 2:
-            for c in packet(n):
-                c.start()
+    send_halo(3)
 
     q_own = q_all[own_rows(0), :]
     q_own32 = q_own.astype(F32)
@@ -527,7 +603,8 @@
             c.wait_recv()
 
     lse, largest = [], []
-    need_ref[...] = functools.reduce(jnp.maximum, [zr_st[i] for i in range(NZ)])
+    most = jnp.max(functools.reduce(jnp.maximum, [zr_st[i][2:3] for i in range(NZ)]))
+    fits_ref[0] = jnp.where(most <= BUDGET, 1, 0)
     for i in range(NZ):
         st = zr_st[i]
         if NEGATIVE[i] % 2 == 1:
@@ -564,9 +641,7 @@
         c.wait()
     for c in infos:
         c.wait_send()
-    for n in range(PACKETS):
-        for c in packet(n):
-            c.wait()
+    finish_halo()
 
 
 def halo_kernel(k_hbm, v_hbm, lowk, lowv, highk, highv, send, recv):
@@ -604,12 +679,10 @@
 
 def resample_kernel(
     packed,
-    anc_ref,
-    low_ref,
-    high_ref,
+    plan_ref,
     att_in,
-    k_hbm,
-    v_hbm,
+    k_in,
+    v_in,
     lowk,
     lowv,
     highk,
@@ -618,92 +691,63 @@
     nk_hbm,
     nv_hbm,
     buf,
-    att_buf,
-    in_sem,
-    out_sem,
+    sem,
 ):
-    first = lax.axis_index("seq") * PART
-    slots = k_hbm.shape[0] * CUT // PART
-    pieces = slots // CUT
-    att = [
-        pltpu.make_async_copy(att_in, att_buf, in_sem.at[2 * PART]),
-        pltpu.make_async_copy(att_buf, att_ref, out_sem.at[2 * PART]),
-    ]
-    att[0].start()
-
-    def places(base, lengths):
-        row, out = 0, []
-        for j in range(HALO):
-            live = lengths(j) // CUT + 1
-            out.append((row if packed else j * pieces, live))
-            wanted = functools.reduce(
-                jnp.maximum, [jnp.where(anc_ref[q] == base + j, 1, 0) for q in range(PART)]
-            )
-            row = row + wanted * live
-        return out
-
-    low = places(first - HALO, lambda j: low_ref[PART - HALO + j, 0])
-    high = places(first + PART, lambda j: high_ref[j, 0])
-
-    def pick(entries, j, which):
-        value = entries[0][which]
-        for n in range(1, HALO):
-            value = jnp.where(j == n, entries[n][which], value)
-        return value
-
-    at = [anc_ref[q] - first for q in range(PART)]
-
-    def fetch(q):
-        local = at[q]
-
-        def start(k, v):
-            pltpu.make_async_copy(k, buf.at[2 * q], in_sem.at[2 * q]).start()
-            pltpu.make_async_copy(v, buf.at[2 * q + 1], in_sem.at[2 * q + 1]).start()
-
-        def side(entries, j, k, v):
-            limit = k.shape[0] - pieces
-            rows = pl.ds(jnp.minimum(jnp.maximum(pick(entries, j, 0), 0), limit), pieces)
-            start(k.at[rows], v.at[rows])
-
-        @pl.when(local < 0)
+    pieces = k_in.shape[0] // PART
+    att = pltpu.make_async_copy(att_in, att_ref, sem.at[2 * PART])
+    att.start()
+    outs = (nk_hbm, nv_hbm)
+
+    def copy(src, begin, out, to, count, i):
+        pltpu.make_async_copy(
+            src.at[pl.ds(begin, count)], out.at[pl.ds(to, count)], sem.at[i]
+        ).start()
+
+    def whole(q, srcs, place):
+        for kind in range(2):
+            limit = srcs[kind].shape[0] // pieces - 1
+            begin = jnp.minimum(jnp.maximum(place, 0), limit) * pieces
+            copy(srcs[kind], begin, outs[kind], q * pieces, pieces, 2 * q + kind)
+
+    def unpack(q, srcs, begin, live):
+        live = jnp.minimum(jnp.maximum(live, 1), pieces)
+        limit = srcs[0].shape[0] - pieces
+        begin = jnp.minimum(jnp.maximum(begin, 0), limit)
+        for kind in range(2):
+            buf[2 * q + kind] = jnp.zeros(buf.shape[1:], BF16)
+
+        def body(n, _):
+            for kind in range(2):
+                buf[2 * q + kind, n] = srcs[kind][begin + n]
+            return 0
+
+        lax.fori_loop(0, live, body, 0)
+        for kind in range(2):
+            i = 2 * q + kind
+            copy(buf.at[i], 0, outs[kind], q * pieces, pieces, i)
+
+    for q in range(PART):
+        side, place = plan_ref[q], plan_ref[PART + q]
+        begin, live = plan_ref[2 * PART + q], plan_ref[3 * PART + q]
+
+        @pl.when(side == 0)
         def _():
-            side(low, local + HALO, lowk, lowv)
-
-        @pl.when(local >= PART)
-        def _():
-            side(high, local - PART, highk, highv)
-
-        @pl.when(jnp.logical_and(local >= 0, local < PART))
-        def _():
-            own = jnp.minimum(jnp.maximum(local, 0), PART - 1)
-            rows = pl.ds(own * pieces, pieces)
-            start(k_hbm.at[rows], v_hbm.at[rows])
+            whole(q, (k_in, v_in), place)
+
+        for n, srcs in ((1, (lowk, lowv)), (2, (highk, highv))):
+
+            @pl.when(side == n)
+            def _():
+                if packed:
+                    unpack(q, srcs, begin, live)
+                else:
+                    whole(q, srcs, place)
 
     for q in range(PART):
-        fetch(q)
-    row = lax.broadcasted_iota(I32, (pieces, CUT, HD), 0)
-    for q in range(PART):
-        local = at[q]
-        for kind, out in ((0, nk_hbm), (1, nv_hbm)):
-            i = 2 * q + kind
-            pltpu.make_async_copy(k_hbm.at[pl.ds(0, pieces)], buf.at[i], in_sem.at[i]).wait()
-            if packed:
-
-                @pl.when(jnp.logical_or(local < 0, local >= PART))
-                def _():
-                    live = jnp.where(
-                        local < 0, pick(low, local + HALO, 1), pick(high, local - PART, 1)
-                    )
-                    buf[i] = jnp.where(row < live, buf[i].astype(F32), 0.0).astype(BF16)
-
-            pltpu.make_async_copy(buf.at[i], out.at[pl.ds(q * pieces, pieces)], out_sem.at[i]).start()
-    att[0].wait()
-    att[1].start()
-    for q in range(PART):
-        for kind, out in ((0, nk_hbm), (1, nv_hbm)):
-            i = 2 * q + kind
-            pltpu.make_async_copy(buf.at[i], out.at[pl.ds(q * pieces, pieces)], out_sem.at[i]).wait()
-    att[1].wait()
+        for kind in range(2):
+            rows = pl.ds(q * pieces, pieces)
+            pltpu.make_async_copy(buf.at[0], outs[kind].at[rows], sem.at[2 * q + kind]).wait()
+    att.wait()
 
 
 def on_device(
@@ -731,9 +775,8 @@
     shape = jax.ShapeDtypeStruct
     window = shape((PART * slots // CUT, CUT, HD), BF16)
     side = shape((BUDGET + slots // CUT, CUT, HD), BF16)
-    info = shape((PART, HD), I32)
     dma = pltpu.SemaphoreType.DMA
-    att, wk, wv, lowk, lowv, highk, highv, low_info, high_info, need = pl.pallas_call(
+    att, wk, wv, lowk, lowv, highk, highv, plan, fits = pl.pallas_call(
         attention_kernel,
         out_shape=(
             shape((PART, GROUP * HD), BF16),
@@ -743,12 +786,11 @@
             side,
             side,
             side,
-            info,
-            info,
-            shape((PART, HD), F32),
+            shape((4 * PART,), I32),
+            shape((1,), I32),
         ),
         in_specs=[hbm] * 9,
-        out_specs=(vmem, hbm, hbm, hbm, hbm, hbm, hbm, vmem, vmem, vmem),
+        out_specs=(vmem, hbm, hbm, hbm, hbm, hbm, hbm, smem, smem),
         scratch_shapes=[
             pltpu.VMEM((TILES * TILE, HD), BF16),
             pltpu.VMEM((keys, HD), BF16),
@@ -761,12 +803,16 @@
             pltpu.SMEM((PART,), I32),
             pltpu.SMEM((PART,), I32),
             pltpu.VMEM((PART, HD), I32),
+            pltpu.VMEM((PART, HD), I32),
+            pltpu.VMEM((PART, HD), I32),
             pltpu.SMEM((PART, HD), I32),
             pltpu.SMEM((PART, HD), I32),
             pltpu.VMEM((BUDGET, CUT, HD), BF16),
             pltpu.VMEM((BUDGET, CUT, HD), BF16),
             pltpu.VMEM((BUDGET, CUT, HD), BF16),
             pltpu.VMEM((BUDGET, CUT, HD), BF16),
+            pltpu.VMEM((CROSS // 2, CUT, HD), BF16),
+            pltpu.VMEM((CROSS // 2, CUT, HD), BF16),
             pltpu.VMEM((TILE, keys), F32),
             pltpu.VMEM((TILE, keys), F32),
             pltpu.VMEM((TILE, HD), F32),
@@ -801,6 +847,8 @@
             dma((2,)),
             dma((PACKETS, 4)),
             dma((PACKETS, 4)),
+            dma((3, 2)),
+            dma((3, 2)),
         ],
         compiler_params=pltpu.CompilerParams(
             collective_id=0, has_side_effects=True, vmem_limit_bytes=VMEM_LIMIT
@@ -816,19 +864,17 @@
                 window,
                 window,
             ),
-            in_specs=[smem, smem, smem] + [hbm] * 7,
+            in_specs=[smem] + [hbm] * 3 + [vmem if packed else hbm] * 4,
             out_specs=(hbm, hbm, hbm),
             scratch_shapes=[
                 pltpu.VMEM((2 * PART, slots // CUT, CUT, HD), BF16),
-                pltpu.VMEM((PART, GROUP * HD), BF16),
-                dma((2 * PART + 1,)),
                 dma((2 * PART + 1,)),
             ],
             compiler_params=pltpu.CompilerParams(vmem_limit_bytes=VMEM_LIMIT),
             name="resample",
         )(*operands)
 
-    def whole(anc, low_info, high_info, att, wk, wv, *_):
+    def whole(plan, att, wk, wv, *_):
         full = shape((HALO * slots // CUT, CUT, HD), BF16)
         sides = pl.pallas_call(
             halo_kernel,
@@ -841,15 +887,13 @@
             ),
             name="halo",
         )(wk, wv)
-        return resample(False, anc, low_info, high_info, att, wk, wv, *sides)
+        return resample(False, plan, att, wk, wv, *sides)
 
     attended, next_keys, next_values = lax.cond(
-        need[2, 0] <= BUDGET,
+        fits[0] > 0,
         functools.partial(resample, True),
         whole,
-        ancestors,
-        low_info,
-        high_info,
+        plan,
         att,
         wk,
         wv,

time: 61.9 us -> 46 us (0.74)
  Pallas kernels: 58.6 us -> 44.6 us
  local copies, waits for them, and re-layouts: 1.84 us -> 0 us
    pallas_call x1, Pallas kernels: 53.3 us -> 42 us  [on_device(): pl.pallas_call(attention_kernel, out_shape=(shape((PART, GROUP * HD), BF1...]
    pallas_call x1, Pallas kernels: 5.31 us -> 2.64 us  [resample(): pl.pallas_call(functools.partial(resample_kernel, packed), out_shape=(sha...]
    slice x1 -> x0, local copies, waits for them, and re-layouts: 1.2 us -> none  [on_device(): need[2, 0] <= BUDGET]
    unnamed x2 -> x0, local copies, waits for them, and re-layouts: 0.65 us -> none
where the time goes in v3:
time: 46 us; the launch traced here: 45.9 us
  Pallas kernels  44.6 us (97%)
  between operations  1.2 us (3%)
    pallas_call x1, Pallas kernels, on_device(): pl.pallas_call(attention_kernel, out_shape=(shape((PART, GROUP * HD), BF1...  42 us
    pallas_call x1, Pallas kernels, resample(): pl.pallas_call(functools.partial(resample_kernel, packed), out_shape=(sha...  2.64 us

profile of v3, /device:TPU:120, one launch (start us, length us, event | category | flops | bytes accessed | tf_op | source)
XLA Modules:
  0.0 45.9 jit_solution(14364321867271395236)
XLA Ops:
  0.6 42.0 %attention.1 = (bf16[8,1024]{1,0:T(8,128)(2,1)S(1)}, bf16[128,32,128]{2,1,0:T(8,128)(2,1)S(1)}, bf16[128,32,128]{2,1,0:T(8,128)(2,1)S(1)}, bf16[60,32,128]{2,1,0...) custom-call(bf16[64,128]{1,0:T(8,128)(2,1)} %bitcast.14, ...), custom_call_target="tpu_custom_call" | custom-call | tf_op jit(solution)/shard_map/attention/pallas_call | solution.py:779
  43.2 2.7 %conditional.1 = ((bf16[8,1024]{1,0:T(8,128)(2,1)}, bf16[128,32,128]{2,1,0:T(8,128)(2,1)}, bf16[128,32,128]{2,1,0:T(8,128)(2,1)})) conditional(s32[]{:T(128)} %bitcast.7, (bf16[128,32,128]{2,1,0:T(8,128)(2,1)S(1)}, bf16[128,32,128]{2,1,0:T(8,128)(2,1)S(1)}, s32[32]{0:T(128)S(1)}, bf16[8,1024]{1,0:T(8,128)(2,1)S(1)}) %tuple.19, (s32[32]{0:T(128)S(1)}, ...), branch_computations={%region_0.0_spmd, %region_1.0_spmd} | conditional | bytes 8 | solution.py:892
  43.2 2.6 %resample.3 = (bf16[8,1024]{1,0:T(8,128)(2,1)}, bf16[128,32,128]{2,1,0:T(8,128)(2,1)}, bf16[128,32,128]{2,1,0:T(8,128)(2,1)}) custom-call(s32[32]{0:T(128)S(1)} %get-tuple-element.43.plan_ref, bf16[8,1024]{1,0:T(8,128)(2,1)S(1)} %get-tuple-element.44.att_in, bf16[128,32,128]{2,1,0:T(8,128)(2,1)S(1)} %get-tuple-element.45.k_in, ...), custom_call_target="tpu_custom_call" | custom-call | tf_op jit(solution)/shard_map/cond/branch_1_fun/resample/pallas_call | solution.py:860

commit v4 on v3

--- a/solution.py
+++ b/solution.py
@@ -445,9 +445,9 @@
 
     def put_stats(ref, lse, largest):
         both = jnp.where(lane == 0, lse, jnp.broadcast_to(largest, lse.shape))
-        for g in range(TILE // HD):
-            st = both[g * HD : (g + 1) * HD].T[:8]
-            ref[g * 8 : (g + 1) * 8, :] = jnp.where(sub == 2, need, st)
+        one, two = [both[g * HD : (g + 1) * HD].T[:8] for g in range(TILE // HD)]
+        rest = jnp.where(sub == 2, need, pltpu.roll(two, 3, 0))
+        ref[...] = jnp.where(sub < 2, one, rest)
 
     def slot_of(n):
         return n + 1 - n // 3 * (4 - 3 * ((5 - n) // 2))
@@ -519,15 +519,15 @@
                 c.wait_recv()
         for g in range(TILE // HD):
             rows = slice(g * HD, (g + 1) * HD)
-            lse = [own_st[half, g * 8 : g * 8 + 1, :]]
+            lse = [own_st[half, 3 * g : 3 * g + 1, :]]
             for j in range(3):
-                lse.append(xr_st[2 * j + half, g * 8 : g * 8 + 1, :])
+                lse.append(xr_st[2 * j + half, 3 * g : 3 * g + 1, :])
             top = functools.reduce(jnp.maximum, lse)
             w = [jnp.exp2(v - top) for v in lse]
             total = functools.reduce(jnp.add, w)
             factors = [w[0] / total]
             for j in range(3):
-                largest = xr_st[2 * j + half, g * 8 + 1 : g * 8 + 2, :]
+                largest = xr_st[2 * j + half, 3 * g + 1 : 3 * g + 2, :]
                 factors.append(w[j + 1] / total * (largest * (1.0 / CODE)))
             cols = turned(factors)
             at = half * TILE + g * HD
@@ -822,11 +822,11 @@
             pltpu.VMEM((ROWS, HD), F32),
             pltpu.VMEM((ROWS, HD), F32),
             pltpu.VMEM((2 * TILE, HD), F32),
-            pltpu.VMEM((2, TILE // 16, HD), F32),
+            pltpu.VMEM((2, 8, HD), F32),
             pltpu.VMEM((6, TILE, HD), I16),
-            pltpu.VMEM((6, TILE // 16, HD), F32),
+            pltpu.VMEM((6, 8, HD), F32),
             pltpu.VMEM((6, TILE, HD), I16),
-            pltpu.VMEM((6, TILE // 16, HD), F32),
+            pltpu.VMEM((6, 8, HD), F32),
             pltpu.VMEM((2 * TILE, HD), I16),
             pltpu.VMEM((4, 8, HD), F32),
             pltpu.VMEM((NZ, ROWS, HD), I16),

time: 46 us -> 45.8 us (level)
  no operation moved by 1% of the time
where the time goes in v4:
time: 45.8 us; the launch traced here: 45.6 us
  Pallas kernels  44.4 us (97%)
  between operations  1.2 us (3%)
    pallas_call x1, Pallas kernels, on_device(): pl.pallas_call(attention_kernel, out_shape=(shape((PART, GROUP * HD), BF1...  41.8 us
    pallas_call x1, Pallas kernels, resample(): pl.pallas_call(functools.partial(resample_kernel, packed), out_shape=(sha...  2.55 us

profile of v4, /device:TPU:120, one launch (start us, length us, event | category | flops | bytes accessed | tf_op | source)
XLA Modules:
  0.0 45.6 jit_solution(1382854873960572703)
XLA Ops:
  0.6 41.8 %attention.1 = (bf16[8,1024]{1,0:T(8,128)(2,1)S(1)}, bf16[128,32,128]{2,1,0:T(8,128)(2,1)S(1)}, bf16[128,32,128]{2,1,0:T(8,128)(2,1)S(1)}, bf16[60,32,128]{2,1,0...) custom-call(bf16[64,128]{1,0:T(8,128)(2,1)} %bitcast.14, ...), custom_call_target="tpu_custom_call" | custom-call | tf_op jit(solution)/shard_map/attention/pallas_call | solution.py:779
  43.0 2.6 %conditional.1 = ((bf16[8,1024]{1,0:T(8,128)(2,1)}, bf16[128,32,128]{2,1,0:T(8,128)(2,1)}, bf16[128,32,128]{2,1,0:T(8,128)(2,1)})) conditional(s32[]{:T(128)} %bitcast.7, (bf16[128,32,128]{2,1,0:T(8,128)(2,1)S(1)}, bf16[128,32,128]{2,1,0:T(8,128)(2,1)S(1)}, s32[32]{0:T(128)S(1)}, bf16[8,1024]{1,0:T(8,128)(2,1)S(1)}) %tuple.19, (s32[32]{0:T(128)S(1)}, ...), branch_computations={%region_0.0_spmd, %region_1.0_spmd} | conditional | bytes 8 | solution.py:892
  43.0 2.6 %resample.3 = (bf16[8,1024]{1,0:T(8,128)(2,1)}, bf16[128,32,128]{2,1,0:T(8,128)(2,1)}, bf16[128,32,128]{2,1,0:T(8,128)(2,1)}) custom-call(s32[32]{0:T(128)S(1)} %get-tuple-element.43.plan_ref, bf16[8,1024]{1,0:T(8,128)(2,1)S(1)} %get-tuple-element.44.att_in, bf16[128,32,128]{2,1,0:T(8,128)(2,1)S(1)} %get-tuple-element.45.k_in, ...), custom_call_target="tpu_custom_call" | custom-call | tf_op jit(solution)/shard_map/cond/branch_1_fun/resample/pallas_call | solution.py:860
